TPU v7x, 32 devices: a whole 2x2x4 slice. The times are simulated.
32 devices in a mesh: groups: 2 (over y), row: 4 (over z), col: 2 (over x), depth: 2 (over core).
Axes of the slice: x: 2, y: 2, z: 4, core: 2. Of those that a mesh axis runs over, the one named last changes fastest.
Arguments:
- density: float32 [512, 4096], P(('groups', 'row', 'col', 'depth')), parts along dimension 0, may hold values from -0.8 to 0.8
- square_left: int32 [32768], P(('groups', 'row', 'col', 'depth')), parts along dimension 0, may hold values from 0 to 63
- square_right: int32 [32768], P(('groups', 'row', 'col', 'depth')), parts along dimension 0, may hold values from 0 to 63
- square_out: int32 [32768], P(('groups', 'row', 'col', 'depth')), parts along dimension 0, may hold values from 0 to 31
- square_count: int32 [32], P(('groups', 'row', 'col', 'depth')), parts along dimension 0, may hold values from 128 to 1024, as said below
- cube_left: int32 [32768], P(('groups', 'row', 'col', 'depth')), parts along dimension 0, may hold values from 0 to 63
- cube_right: int32 [32768], P(('groups', 'row', 'col', 'depth')), parts along dimension 0, may hold values from 0 to 63
- cube_out: int32 [32768], P(('groups', 'row', 'col', 'depth')), parts along dimension 0, may hold values from 0 to 31
- cube_count: int32 [32], P(('groups', 'row', 'col', 'depth')), parts along dimension 0, may hold values from 128 to 1024, as said below
Outputs:
- purified: float32 [512, 4096], P(('groups', 'row', 'col', 'depth')), parts along dimension 0
There are 2 independent parts, one for each index of `groups`. A program takes and returns all parts, laid end to end along the dimension named above; each array names one. Nothing has to cross between parts.
Inputs may be any that keep to these rules, and one draw needn't show every extreme that they name: `square_count`: each device has an eighth, a quarter, a half or all of 1024 live tasks, and some device of every copy has all 1024. `cube_count`: as for square_count.
All inputs are finite; a program needn't handle non-finite values.
Results may differ from a plain program's by a relative error of at most 0.0003.
Values sent between devices are 32-bit elements; how exact they have to be, the bound alone decides.
No kernel may reach another device: no remote copies, remote signals or barrier semaphores. Data moves between devices by JAX's collectives and lax.ppermute only.
A program may use at most 64 MiB of HBM per device.

v0:
```python
import math

import jax
import jax.numpy as jnp
from jax import lax
from jax.sharding import PartitionSpec as P

OUT_DEV = 16


def tile_sum(left, right, left_index, right_index, out_index, count, slots):
    tasks = left_index.shape[0]
    width = left.shape[1]
    side = math.isqrt(width)
    stride = min(128, tasks)
    turns = (count + stride - 1) // stride

    def turn(index, total):
        start = index * stride
        lefts = lax.dynamic_slice_in_dim(left_index, start, stride)
        rights = lax.dynamic_slice_in_dim(right_index, start, stride)
        outs = lax.dynamic_slice_in_dim(out_index, start, stride)
        first = jnp.take(left, lefts, axis=0).reshape(stride, side, side)
        second = jnp.take(right, rights, axis=0).reshape(stride, side, side)
        product = jnp.einsum(
            "tij,tjk->tik", first, second, precision=lax.Precision.HIGHEST
        ).reshape(stride, width)
        live = (start + jnp.arange(stride, dtype=jnp.int32) < count).astype(jnp.float32)
        onehot = (outs[:, None] == jnp.arange(slots, dtype=jnp.int32)[None, :]).astype(
            jnp.float32
        ) * live[:, None]
        return total + jnp.dot(onehot.T, product, precision=lax.Precision.HIGHEST)

    return lax.fori_loop(0, turns, turn, jnp.zeros((slots, width), jnp.float32))


def local(
    density,
    square_left,
    square_right,
    square_out,
    square_count,
    cube_left,
    cube_right,
    cube_out,
    cube_count,
):
    layers = lax.axis_size("depth")
    slots = layers * OUT_DEV
    row_blocks = lax.all_gather(density, ("col", "depth"), axis=0, tiled=True)
    column_blocks = lax.all_gather(density, "row", axis=0, tiled=True)
    partial_value = tile_sum(
        row_blocks, column_blocks, square_left, square_right, square_out, square_count[0], slots
    )
    square = lax.psum_scatter(partial_value, "depth", scatter_dimension=0, tiled=True)
    square_blocks = lax.all_gather(square, ("col", "depth"), axis=0, tiled=True)
    cube_part = tile_sum(
        square_blocks, column_blocks, cube_left, cube_right, cube_out, cube_count[0], slots
    )
    cube = lax.psum_scatter(cube_part, "depth", scatter_dimension=0, tiled=True)
    return 3.0 * square - 2.0 * cube


def solution(mesh):
    return jax.shard_map(
        local,
        mesh=mesh,
        in_specs=(
            P(("groups", "row", "col", "depth"), None),
            P(("groups", "row", "col", "depth")),
            P(("groups", "row", "col", "depth")),
            P(("groups", "row", "col", "depth")),
            P(("groups", "row", "col", "depth")),
            P(("groups", "row", "col", "depth")),
            P(("groups", "row", "col", "depth")),
            P(("groups", "row", "col", "depth")),
            P(("groups", "row", "col", "depth")),
        ),
        out_specs=P(("groups", "row", "col", "depth"), None),
        check_vma=False,
    )
```

profile of v0, /device:TPU:0, one launch (start us, length us, event | category | flops | bytes accessed | tf_op | source)
XLA Modules:
  0.0 821.6 jit_solution(367571823912803276)
XLA Ops:
  8.7 19.6 %all-gather.4.cloned.1.call-done = f32[64,4096]{1,0:T(8,128)} async-done(((f32[16,4096]{1,0:T(8,128)}), f32[64,4096]{1,0:T(8,128)}) %all-gather.4.cloned.1.call-update) | async-done | bytes 1048592 | tf_op jit(solution)/shard_map/all_gather | solution.py:50
  28.4 29.5 %all-gather.6.cloned.1.call-done = f32[64,4096]{1,0:T(8,128)} async-done(((f32[16,4096]{1,0:T(8,128)}), f32[64,4096]{1,0:T(8,128)}) %all-gather.6.cloned.1.call-update) | async-done | bytes 1048592 | tf_op jit(solution)/shard_map/all_gather | solution.py:51
  58.7 179.6 %while.20 = (s32[]{:T(128)}, f32[32,4096]{1,0:T(8,128)}, s32[]{:T(128)}, s32[1024]{0:T(1024)}, s32[]{:T(128)}, /*index=5*/s32[1024]{0:T(1024)}, f32[64,4096]{1,0...) while((s32[]{:T(128)}, f32[32,4096]{1,0:T(8,128)}, ...), condition=%wide.region_1.3_spmd, body=%wide.region_0.2_spmd.sunk | while | flops 605171584 | bytes 55590160 | solution.py:34
  61.0 3.5 gather_fusion.1
  76.7 5.6 copy.31
  82.3 4.5 copy.33
  86.8 9.8 %fusion.32 = f32[128,64,64]{2,1,0:T(8,128)} fusion(f32[128,64,64]{2,1,0:T(8,128)} %copy.31, f32[128,64,64]{2,1,0:T(8,128)} %copy.33), kind=kOutput, calls=%fused_computation.37.clone.1 | convolution fusion | flops 402653184 | bytes 6291456 | tf_op jit(solution)/shard_map/while/body/tij,tjk->tik/dot_general | solution.py:25
  96.6 3.9 copy.34
  105.9 3.5 gather_fusion.1
  121.6 5.6 copy.31
  127.2 4.5 copy.33
  131.7 9.8 %fusion.32 = f32[128,64,64]{2,1,0:T(8,128)} fusion(f32[128,64,64]{2,1,0:T(8,128)} %copy.31, f32[128,64,64]{2,1,0:T(8,128)} %copy.33), kind=kOutput, calls=%fused_computation.37.clone.1 | convolution fusion | flops 402653184 | bytes 6291456 | tf_op jit(solution)/shard_map/while/body/tij,tjk->tik/dot_general | solution.py:25
  141.6 3.9 copy.34
  150.8 3.5 gather_fusion.1
  166.5 5.6 copy.31
  172.1 4.5 copy.33
  176.6 9.8 %fusion.32 = f32[128,64,64]{2,1,0:T(8,128)} fusion(f32[128,64,64]{2,1,0:T(8,128)} %copy.31, f32[128,64,64]{2,1,0:T(8,128)} %copy.33), kind=kOutput, calls=%fused_computation.37.clone.1 | convolution fusion | flops 402653184 | bytes 6291456 | tf_op jit(solution)/shard_map/while/body/tij,tjk->tik/dot_general | solution.py:25
  186.5 3.9 copy.34
  195.7 3.5 gather_fusion.1
  211.4 5.6 copy.31
  217.0 4.5 copy.33
  221.5 9.8 %fusion.32 = f32[128,64,64]{2,1,0:T(8,128)} fusion(f32[128,64,64]{2,1,0:T(8,128)} %copy.31, f32[128,64,64]{2,1,0:T(8,128)} %copy.33), kind=kOutput, calls=%fused_computation.37.clone.1 | convolution fusion | flops 402653184 | bytes 6291456 | tf_op jit(solution)/shard_map/while/body/tij,tjk->tik/dot_general | solution.py:25
  231.4 3.9 copy.34
  238.5 187.2 %reduce-scatter.3.cloned.1.call-done = f32[16,4096]{1,0:T(8,128)} async-done(((f32[32,4096]{1,0:T(8,128)}), f32[16,4096]{1,0:T(8,128)}) %reduce-scatter.3.cloned.1.call-update) | async-done | bytes 262160 | tf_op jit(solution)/shard_map/reduce_scatter | solution.py:55
  426.4 18.7 %all-gather.8.cloned.1.call-done = f32[64,4096]{1,0:T(8,128)} async-done(((f32[16,4096]{1,0:T(8,128)}), f32[64,4096]{1,0:T(8,128)}) %all-gather.8.cloned.1.call-update) | async-done | bytes 1048592 | tf_op jit(solution)/shard_map/all_gather | solution.py:56
  445.9 359.3 %while.21 = (s32[]{:T(128)}, f32[32,4096]{1,0:T(8,128)}, s32[]{:T(128)}, s32[1024]{0:T(1024)}, s32[]{:T(128)}, /*index=5*/s32[1024]{0:T(1024)}, f32[64,4096]{1,0...) while((s32[]{:T(128)}, f32[32,4096]{1,0:T(8,128)}, ...), condition=%wide.region_4.6_spmd, body=%wide.region_3.5_spmd.sunk | while | flops 605171584 | bytes 55590160 | solution.py:34
  448.2 3.5 gather_fusion.3
  463.9 5.6 copy.36
  469.5 4.5 copy.38
  474.0 9.8 %fusion.37 = f32[128,64,64]{2,1,0:T(8,128)} fusion(f32[128,64,64]{2,1,0:T(8,128)} %copy.36, f32[128,64,64]{2,1,0:T(8,128)} %copy.38), kind=kOutput, calls=%fused_computation.38.clone.1 | convolution fusion | flops 402653184 | bytes 6291456 | tf_op jit(solution)/shard_map/while/body/tij,tjk->tik/dot_general | solution.py:25
  483.8 3.9 copy.39
  493.1 3.5 gather_fusion.3
  508.8 5.6 copy.36
  514.4 4.5 copy.38
  518.9 9.8 %fusion.37 = f32[128,64,64]{2,1,0:T(8,128)} fusion(f32[128,64,64]{2,1,0:T(8,128)} %copy.36, f32[128,64,64]{2,1,0:T(8,128)} %copy.38), kind=kOutput, calls=%fused_computation.38.clone.1 | convolution fusion | flops 402653184 | bytes 6291456 | tf_op jit(solution)/shard_map/while/body/tij,tjk->tik/dot_general | solution.py:25
  528.8 3.9 copy.39
  538.0 3.5 gather_fusion.3
  553.7 5.6 copy.36
  559.3 4.5 copy.38
  563.8 9.8 %fusion.37 = f32[128,64,64]{2,1,0:T(8,128)} fusion(f32[128,64,64]{2,1,0:T(8,128)} %copy.36, f32[128,64,64]{2,1,0:T(8,128)} %copy.38), kind=kOutput, calls=%fused_computation.38.clone.1 | convolution fusion | flops 402653184 | bytes 6291456 | tf_op jit(solution)/shard_map/while/body/tij,tjk->tik/dot_general | solution.py:25
  573.7 3.9 copy.39
  582.9 3.5 gather_fusion.3
  598.6 5.6 copy.36
  604.2 4.5 copy.38
  608.7 9.8 %fusion.37 = f32[128,64,64]{2,1,0:T(8,128)} fusion(f32[128,64,64]{2,1,0:T(8,128)} %copy.36, f32[128,64,64]{2,1,0:T(8,128)} %copy.38), kind=kOutput, calls=%fused_computation.38.clone.1 | convolution fusion | flops 402653184 | bytes 6291456 | tf_op jit(solution)/shard_map/while/body/tij,tjk->tik/dot_general | solution.py:25
  618.6 3.9 copy.39
  643.5 5.6 copy.36
  649.1 4.5 copy.38
  653.6 9.8 %fusion.37 = f32[128,64,64]{2,1,0:T(8,128)} fusion(f32[128,64,64]{2,1,0:T(8,128)} %copy.36, f32[128,64,64]{2,1,0:T(8,128)} %copy.38), kind=kOutput, calls=%fused_computation.38.clone.1 | convolution fusion | flops 402653184 | bytes 6291456 | tf_op jit(solution)/shard_map/while/body/tij,tjk->tik/dot_general | solution.py:25
  663.5 3.9 copy.39
  672.7 3.5 gather_fusion.3
  688.4 5.6 copy.36
  694.0 4.5 copy.38
  698.6 9.8 %fusion.37 = f32[128,64,64]{2,1,0:T(8,128)} fusion(f32[128,64,64]{2,1,0:T(8,128)} %copy.36, f32[128,64,64]{2,1,0:T(8,128)} %copy.38), kind=kOutput, calls=%fused_computation.38.clone.1 | convolution fusion | flops 402653184 | bytes 6291456 | tf_op jit(solution)/shard_map/while/body/tij,tjk->tik/dot_general | solution.py:25
  708.4 3.9 copy.39
  733.4 5.6 copy.36
  738.9 4.5 copy.38
  743.5 9.8 %fusion.37 = f32[128,64,64]{2,1,0:T(8,128)} fusion(f32[128,64,64]{2,1,0:T(8,128)} %copy.36, f32[128,64,64]{2,1,0:T(8,128)} %copy.38), kind=kOutput, calls=%fused_computation.38.clone.1 | convolution fusion | flops 402653184 | bytes 6291456 | tf_op jit(solution)/shard_map/while/body/tij,tjk->tik/dot_general | solution.py:25
  753.3 3.9 copy.39
  778.3 5.6 copy.36
  783.8 4.5 copy.38
  788.4 9.8 %fusion.37 = f32[128,64,64]{2,1,0:T(8,128)} fusion(f32[128,64,64]{2,1,0:T(8,128)} %copy.36, f32[128,64,64]{2,1,0:T(8,128)} %copy.38), kind=kOutput, calls=%fused_computation.38.clone.1 | convolution fusion | flops 402653184 | bytes 6291456 | tf_op jit(solution)/shard_map/while/body/tij,tjk->tik/dot_general | solution.py:25
  798.2 3.9 copy.39
  805.2 8.1 reduce-scatter.5.cloned.1.call-done
  (222 shorter events, 226.3 us)
Async XLA Ops:
  6.5 21.8 %all-gather.4.cloned.1.call-start = ((), (), s32[]{:S(2)}) async-start(), calls=%async_computation.2 | async-start | bytes 1310720 | tf_op jit(solution)/shard_map/all_gather | solution.py:50
  7.3 50.7 %all-gather.6.cloned.1.call-start = ((), (), s32[]{:S(2)}) async-start(), calls=%async_computation.3 | async-start | bytes 1310720 | tf_op jit(solution)/shard_map/all_gather | solution.py:51
  8.0 417.6 %reduce-scatter.3.cloned.1.call-start = ((), (), s32[]{:S(2)}) async-start(), calls=%async_computation.4 | async-start | bytes 786432 | tf_op jit(solution)/shard_map/reduce_scatter | solution.py:55
  66.0 2.0 copy-start
  96.6 3.9 copy-start.4
  102.9 0.8 copy-start.5
  110.9 2.0 copy-start
  141.6 3.9 copy-start.4
  147.8 0.8 copy-start.5
  155.9 2.0 copy-start
  186.5 3.9 copy-start.4
  192.7 0.8 copy-start.5
  200.8 2.0 copy-start
  231.4 3.9 copy-start.4
  237.6 0.8 copy-start.5
  238.4 206.6 %all-gather.8.cloned.1.call-start = ((), (), s32[]{:S(2)}) async-start(), calls=%async_computation.5 | async-start | bytes 1310720 | tf_op jit(solution)/shard_map/all_gather | solution.py:56
  425.7 387.7 %reduce-scatter.5.cloned.1.call-start = ((), (), s32[]{:S(2)}) async-start(), calls=%async_computation.6 | async-start | bytes 786432 | tf_op jit(solution)/shard_map/reduce_scatter | solution.py:60
  445.9 367.5 %copy-start.6 = (f32[16,4096]{1,0:T(8,128)S(1)}, f32[16,4096]{1,0:T(8,128)}, u32[]{:S(2)}) copy-start(f32[16,4096]{1,0:T(8,128)} %reduce-scatter.3.cloned.1.call-done) | copy-start | bytes 786436
  453.2 2.0 copy-start.1
  483.8 3.9 copy-start.2
  490.0 0.8 copy-start.3
  498.1 2.0 copy-start.1
  528.7 3.9 copy-start.2
  535.0 0.8 copy-start.3
  543.0 2.0 copy-start.1
  573.7 3.9 copy-start.2
  579.9 0.8 copy-start.3
  588.0 2.0 copy-start.1
  618.6 3.9 copy-start.2
  624.8 0.8 copy-start.3
  632.9 2.0 copy-start.1
  663.5 3.9 copy-start.2
  669.7 0.8 copy-start.3
  677.8 2.0 copy-start.1
  708.4 3.9 copy-start.2
  714.6 0.8 copy-start.3
  722.7 2.0 copy-start.1
  753.3 3.9 copy-start.2
  759.5 0.8 copy-start.3
  767.6 2.0 copy-start.1
  798.2 3.9 copy-start.2
  804.4 0.8 copy-start.3
Sparse Core Ops, SparseCore 0:
  8.9 19.4 all-gather.3
  29.9 27.9 all-gather.5
  238.5 187.0 reduce-scatter.2
  427.1 17.8 all-gather.7
  805.4 7.9 reduce-scatter.4
where the time goes:
time: 825 us; the launch traced here: 822 us
  local copies, waits for them, and re-layouts  319 us (39%)
  waiting for transfers between devices  265 us (32%)
  matrix products  146 us (18%)
  other arithmetic  76.4 us (9%)
  between operations  14.5 us (2%)
    reduce_scatter x1, waiting for transfers between devices, local(): lax.psum_scatter(partial_value, 'depth', scatter_dimension=0, tiled=True)  187 us
    dot_general x12, matrix products, turn(): jnp.einsum('tij,tjk->tik', first, second, precision=lax.Precision.HIGHEST)  118 us
    reshape x12, local copies, waits for them, and re-layouts, turn(): first = jnp.take(left, lefts, axis=0).reshape(stride, side, side)  66.7 us
    reshape x12, local copies, waits for them, and re-layouts, turn(): second = jnp.take(right, rights, axis=0).reshape(stride, side, side)  54.6 us
    dot_general x12, local copies, waits for them, and re-layouts, turn(): jnp.einsum('tij,tjk->tik', first, second, precision=lax.Precision.HIGHEST)  46.3 us
    gather x12, local copies, waits for them, and re-layouts, turn(): second = jnp.take(right, rights, axis=0).reshape(stride, side, side)  41.5 us
    select_n x12, other arithmetic, turn(): first = jnp.take(left, lefts, axis=0).reshape(stride, side, side)  38.2 us
    select_n x12, local copies, waits for them, and re-layouts, turn(): first = jnp.take(left, lefts, axis=0).reshape(stride, side, side)  35 us
  transfers between devices with their start and end apart: 5, of which 5 were waited for; matrix products, arithmetic and copies ran while one was open for 0% of the time, Pallas kernels for 0%

commit v1 on v0

v1 whole, which is shorter than its diff:
```python
import functools
import math

import jax
import jax.numpy as jnp
from jax import lax
from jax.experimental import pallas as pl
from jax.experimental.pallas import tpu as pltpu
from jax.sharding import PartitionSpec as P

OUT_DEV = 16
CHUNK = 8
TURN = 4


def ring(value, axis):
    size = lax.axis_size(axis)
    return lax.ppermute(value, axis, [(i, (i + 1) % size) for i in range(size)])


def ring_all(value, axis):
    pieces = [value]
    for _ in range(lax.axis_size(axis) - 1):
        pieces.append(ring(pieces[-1], axis))
    return pieces


def plan(key, left, out, groups, seg_groups, slots, chunks):
    tasks = key.shape[0]
    place = jnp.arange(tasks, dtype=jnp.int32)
    group = jnp.arange(groups, dtype=jnp.int32)
    segs = groups // seg_groups
    same = (key[:, None] == key[None, :]) & (place[:, None] < place[None, :])
    rank = jnp.sum(same.astype(jnp.int32), axis=0)
    count = jnp.sum((key[:, None] == group[None, :]).astype(jnp.int32), axis=0)
    filled = (count + CHUNK - 1) // CHUNK
    seg_id = group // seg_groups
    earlier = (group[:, None] < group[None, :]) & (seg_id[:, None] == seg_id[None, :])
    within = jnp.sum(jnp.where(earlier, filled[:, None], 0), axis=0)
    total = jnp.sum(filled.reshape(segs, seg_groups), axis=1)
    turns = (total + TURN - 1) // TURN
    seg = jnp.arange(segs, dtype=jnp.int32)
    first = jnp.sum(jnp.where(seg[:, None] < seg[None, :], turns[:, None], 0), axis=0)
    base = within + TURN * jnp.sum(
        jnp.where(seg_id[:, None] == seg[None, :], first[None, :], 0), axis=1
    )
    start = jnp.sum(jnp.where(key[:, None] == group[None, :], base[None, :] * CHUNK, 0), axis=1)
    position = jnp.where(key < groups, start + rank, -1)
    slot = jnp.arange(chunks * CHUNK, dtype=jnp.int32)
    code = jnp.sum(
        jnp.where(
            position[:, None] == slot[None, :], (left * (slots + 1) + out - slots)[:, None], 0
        ),
        axis=0,
    ) + slots
    chunk = jnp.arange(chunks, dtype=jnp.int32)
    rights = jnp.sum((base + filled)[:, None] <= chunk[None, :], axis=0, dtype=jnp.int32)
    return dict(
        first=first,
        turns=turns,
        rights=rights,
        left=code // (slots + 1) * 32,
        out=code % (slots + 1) * 32,
    )


def kernel(raw_lefts, raw_rights, has_left, has_right, has_sum, last, slots, first_group, refs):
    refs = list(refs)
    meta, rights, lefts, outs = refs[:4]
    refs = refs[4:]
    left_raw, refs = refs[:raw_lefts], refs[raw_lefts:]
    right_raw, refs = refs[:raw_rights], refs[raw_rights:]
    panel, given, sum_in = None, [], None
    if has_left:
        panel, refs = refs[0], refs[1:]
    given, refs = refs[:has_right], refs[has_right:]
    if has_sum:
        sum_in, refs = refs[0], refs[1:]
    results, refs = refs[:2] if last else refs[:1], refs[2:] if last else refs[1:]
    if raw_lefts:
        panel, refs = refs[0], refs[1:]
    if raw_rights:
        weights, refs = refs[0], refs[1:]
    else:
        weights = given[0]
    flat, tall, sum_0, sum_1 = refs
    sums = (sum_0, sum_1)
    low = lax.broadcasted_iota(jnp.int32, (32, 128), 1) < 64

    def spread(source):
        for high in range(0, source.shape[0], 8):
            for pair in range(32):
                flat[pl.ds(high * 32 + pair, 8, stride=32), :] = source[
                    high : high + 8, pair * 128 : pair * 128 + 128
                ]

    def split(value):
        top = value.astype(jnp.bfloat16)
        return top, (value - top.astype(jnp.float32)).astype(jnp.bfloat16)

    for index, source in enumerate(left_raw):
        spread(source)
        for block in range(16):
            top, rest = split(flat[block * 32 : block * 32 + 32, :])
            panel[pl.ds(index * 512 + block * 32, 32), 0:128] = top
            panel[pl.ds(index * 512 + block * 32, 32), 128:256] = rest
    for index, source in enumerate(right_raw):
        spread(source)
        for block in range(16):
            both = flat[block * 32 : block * 32 + 32, :]
            swapped = pltpu.roll(both, 64, 1)
            spot = block % 4 * 128
            tall[pl.ds(spot, 32, stride=2), :] = jnp.where(low, both, 0.0)
            tall[pl.ds(spot + 1, 32, stride=2), :] = jnp.where(low, swapped, 0.0)
            tall[pl.ds(spot + 64, 32, stride=2), :] = jnp.where(low, 0.0, swapped)
            tall[pl.ds(spot + 65, 32, stride=2), :] = jnp.where(low, 0.0, both)
            top, rest = split(tall[spot : spot + 128, :])
            weights[index * 16 + block, 0] = top
            weights[index * 16 + block, 1] = rest

    sum_1[...] = jnp.zeros_like(sum_1)
    if has_sum:
        sum_0[...] = sum_in[...]
    else:
        sum_0[...] = jnp.zeros_like(sum_0)

    zero = jnp.zeros((128, 128), jnp.bfloat16)
    limit = weights.shape[0] - 1
    most = panel.shape[0] - 32

    def issue(chunk, unit, total):
        right = jnp.clip(rights[chunk] - first_group, 0, limit)
        top, rest = weights[right, 0], weights[right, 1]
        pltpu.matmul_push_rhs(
            jnp.concatenate(
                [jnp.concatenate([top, rest], 1), jnp.concatenate([top, zero], 1)], 0
            ),
            0,
            unit,
        )
        rows = [
            panel[pl.ds(pl.multiple_of(jnp.minimum(lefts[chunk * CHUNK + task], most), 32), 32), :]
            for task in range(CHUNK)
        ]
        pltpu.matmul_acc_lhs(total, jnp.concatenate(rows, 0), load_staged_rhs=0)

    def drain(chunk, unit, total):
        product = pltpu.matmul_pop(total)
        product = product[:, :128] + product[:, 128:]
        for task in range(CHUNK):
            rows = pl.ds(pl.multiple_of(outs[chunk * CHUNK + task], 32), 32)
            sums[unit][rows, :] += product[task * 32 : task * 32 + 32]

    def work(*totals):
        begin, turns = meta[0] * TURN, meta[1]
        for unit in range(2):
            issue(begin + unit, unit, totals[unit])

        @pl.loop(0, turns)
        def _(turn):
            chunk = begin + turn * TURN
            for unit in range(2):
                issue(chunk + 2 + unit, unit, totals[2 + unit])
            for unit in range(2):
                drain(chunk + unit, unit, totals[unit])
            for unit in range(2):
                issue(chunk + 4 + unit, unit, totals[unit])
            for unit in range(2):
                drain(chunk + 2 + unit, unit, totals[2 + unit])

        for unit in range(2):
            pltpu.matmul_pop(totals[unit])

    pl.run_scoped(
        work,
        *[pltpu.ACC(unit)((CHUNK * 32, 256), jnp.float32) for _ in range(2) for unit in range(2)],
    )

    if not last:
        results[0][...] = sum_0[...] + sum_1[...]
        return
    sum_0[...] = sum_0[...] + sum_1[...]
    layer = meta[2]
    size = results[0].shape[0]
    layers = slots // size
    for index, result in enumerate(results):
        row = (layer * size if index == 0 else lax.rem(layer + 1, layers) * size) * 32
        for high in range(0, size, 8):
            for pair in range(32):
                result[high : high + 8, pair * 128 : pair * 128 + 128] = sum_0[
                    pl.ds(row + high * 32 + pair, 8, stride=32), :
                ]


def tile_sum(tasks, seg, seg_count, left_raw, right_raw, panel, given, sum_in, last, slots, width, first_group):
    f32, bf16 = jnp.float32, jnp.bfloat16
    turns = tasks["turns"][seg]
    for other in range(seg + 1, seg + seg_count):
        turns = turns + tasks["turns"][other]
    meta = jnp.stack([tasks["first"][seg], turns, lax.axis_index("depth")]).astype(jnp.int32)
    args = [meta, tasks["rights"], tasks["left"], tasks["out"], *left_raw, *right_raw]
    smem, vmem = pl.BlockSpec(memory_space=pltpu.SMEM), pl.BlockSpec(memory_space=pltpu.VMEM)
    extra = [v for v in [panel, *given, sum_in] if v is not None]
    in_specs = [smem] * 4 + [vmem] * (len(left_raw) + len(right_raw) + len(extra))
    sum_shape = ((slots + 1) * 32, 128)
    shapes = (
        [jax.ShapeDtypeStruct((OUT_DEV, width), f32)] * 2
        if last
        else [jax.ShapeDtypeStruct(sum_shape, f32)]
    )
    if left_raw:
        shapes.append(jax.ShapeDtypeStruct((len(left_raw) * 512, 256), bf16))
    if right_raw:
        shapes.append(jax.ShapeDtypeStruct((len(right_raw) * 16, 2, 128, 128), bf16))
    body = functools.partial(
        kernel,
        len(left_raw),
        len(right_raw),
        panel is not None,
        len(given),
        sum_in is not None,
        last,
        slots,
        first_group,
    )
    return pl.pallas_call(
        lambda *refs: body(refs),
        out_shape=shapes,
        in_specs=in_specs,
        out_specs=[vmem] * len(shapes),
        scratch_shapes=[
            pltpu.VMEM((512, 128), f32),
            pltpu.VMEM((512, 128), f32),
            pltpu.VMEM(sum_shape, f32),
            pltpu.VMEM(sum_shape, f32),
        ],
        compiler_params=pltpu.CompilerParams(vmem_limit_bytes=44 << 20),
    )(*args, *extra)


def local(
    density,
    square_left,
    square_right,
    square_out,
    square_count,
    cube_left,
    cube_right,
    cube_out,
    cube_count,
):
    per_dev, width = density.shape
    rows, cols, layers = (lax.axis_size(name) for name in ("row", "col", "depth"))
    row, col, layer = (lax.axis_index(name) for name in ("row", "col", "depth"))
    slots = layers * OUT_DEV
    tasks = square_left.shape[0]
    place = jnp.arange(tasks, dtype=jnp.int32)

    def moved_left(left):
        from_col = lax.rem(col - left // (layers * per_dev) + cols, cols)
        from_layer = lax.rem(layer - left // per_dev % layers + layers, layers)
        return from_col, (from_col * layers + from_layer) * per_dev + left % per_dev

    def moved_right(right):
        return lax.rem(row - right // per_dev + rows, rows) * per_dev + right % per_dev

    column = ring_all(density, "row")
    across = ring_all(density, "col")
    lefts = [piece for value in across for piece in ring_all(value, "depth")]

    groups = rows * per_dev
    _, left = moved_left(square_left)
    key = jnp.where(place < square_count[0], moved_right(square_right), groups)
    chunks = -(-(tasks // CHUNK + groups + TURN * rows + TURN) // 16) * 16
    square_tasks = plan(key, left, square_out, groups, per_dev, slots, chunks)
    from_col, left = moved_left(cube_left)
    left = left - jnp.where(from_col == 0, 0, layers * per_dev)
    key = jnp.where(from_col == 0, 0, groups) + moved_right(cube_right)
    key = jnp.where(place < cube_count[0], key, 2 * groups)
    chunks = -(-(tasks // CHUNK + 2 * groups + TURN * 2 + TURN) // 16) * 16
    cube_tasks = plan(key, left, cube_out, 2 * groups, groups, slots, chunks)

    total, panel, first = tile_sum(
        square_tasks, 0, 2, lefts, column[:2], None, [], None, False, slots, width, 0
    )
    weights = [first]
    for seg in range(2, rows):
        *result, piece = tile_sum(
            square_tasks, seg, 1, [], [column[seg]], panel, [], total, seg == rows - 1,
            slots, width, seg * per_dev,
        )
        total = result[0]
        weights.append(piece)
    mine, other = result
    weights = jnp.concatenate(weights, axis=0)
    square = mine + ring(other, "depth")

    squares = [piece for value in ring_all(square, "col") for piece in ring_all(value, "depth")]
    total, near = tile_sum(
        cube_tasks, 0, 1, squares[:layers], [], None, [weights], None, False, slots, width, 0
    )
    mine, other, _ = tile_sum(
        cube_tasks, 1, 1, squares[layers:], [], None, [weights], total, True, slots, width, groups
    )
    cube = mine + ring(other, "depth")
    return 3.0 * square - 2.0 * cube


def solution(mesh):
    return jax.shard_map(
        local,
        mesh=mesh,
        in_specs=(
            P(("groups", "row", "col", "depth"), None),
            P(("groups", "row", "col", "depth")),
            P(("groups", "row", "col", "depth")),
            P(("groups", "row", "col", "depth")),
            P(("groups", "row", "col", "depth")),
            P(("groups", "row", "col", "depth")),
            P(("groups", "row", "col", "depth")),
            P(("groups", "row", "col", "depth")),
            P(("groups", "row", "col", "depth")),
        ),
        out_specs=P(("groups", "row", "col", "depth"), None),
        check_vma=False,
    )
```

time: 825 us -> 73.5 us (0.09)
  the two profiles are of different devices: /device:TPU:0 before, /device:TPU:3 now
where the time goes in v1:
time: 73.5 us; the launch traced here: 73.2 us
  Pallas kernels  25.9 us (35%)
  starting transfers between devices  14.9 us (20%)
  other arithmetic  13.3 us (18%)
  waiting for transfers between devices  12.3 us (17%)
  local copies, waits for them, and re-layouts  4.19 us (6%)
  between operations  2.67 us (4%)
    pallas_call x5, Pallas kernels, tile_sum(): pl.pallas_call(lambda *refs: body(refs), out_shape=shapes, in_specs=in_sp...  25.9 us
    ppermute x11, starting transfers between devices, ring(): return lax.ppermute(value, axis, [(i, (i + 1) % size) for i in range(size)])  14.9 us
    ppermute x11, waiting for transfers between devices, ring(): return lax.ppermute(value, axis, [(i, (i + 1) % size) for i in range(size)])  12.3 us
    another operation x5, other arithmetic, tile_sum(): jnp.stack([tasks['first'][seg], turns, lax.axis_index('depth')])  6.04 us
    reduce_sum x2, other arithmetic, plan(): jnp.sum(jnp.where(position[:, None] == slot[None, :], (left * (slots + 1)...  2.22 us
    sub x2, other arithmetic, plan(): left * (slots + 1) + out - slots  1.51 us
  transfers between devices with their start and end apart: 11, of which 3 were waited for; matrix products, arithmetic and copies ran while one was open for 22% of the time, Pallas kernels for 21%

profile of v1, /device:TPU:3, one launch (start us, length us, event | category | flops | bytes accessed | tf_op | source)
XLA Modules:
  0.0 73.2 jit_solution(9417726187710276734)
XLA Ops:
  0.0 1.3 %collective-permute-start = (f32[16,4096]{1,0:T(8,128)}, f32[16,4096]{1,0:T(8,128)S(1)}, u32[]{:S(2)}, u32[]{:S(2)}) collective-permute-start(f32[16,4096]{1,0:T(8,128)} %refs_8_.1), channel_id=1, source_target_pairs={{0,4},{4,8},{8,12},{12,0},{1,5},{5,9},{9,13},{13,1},{2,6},{6,10},{... | collective-permute-start | bytes 786440 | tf_op jit(solution)/shard_map/ppermute | solution.py:18
  1.3 1.0 %collective-permute-start.3 = (f32[16,4096]{1,0:T(8,128)}, f32[16,4096]{1,0:T(8,128)S(1)}, u32[]{:S(2)}, u32[]{:S(2)}) collective-permute-start(f32[16,4096]{1,0:T(8,128)} %refs_8_.1), channel_id=1, source_target_pairs={{0,1},{1,0},{2,3},{3,2},{4,5},{5,4},{6,7},{7,6},{8,9},{9,8},{10,11... | collective-permute-start | bytes 786440 | tf_op jit(solution)/shard_map/ppermute | solution.py:18
  2.3 0.3 collective-permute-start.4
  3.8 0.8 %fusion.51 = (s32[1024]{0:T(1024)S(1)}, s32[1024]{0:T(1024)S(1)}, s32[1024]{0:T(1024)S(1)}) fusion(s32[1024]{0:T(1024)} %param.16, s32[1024]{0:T(1024)} %param.14, s32[]{:T(128)} %axis_index.23, s32[]{:T(128)S(6)} %axis_index.26, s32[1024]{0:T(1024)} %param.15, s32[]{:T(128)S(6)} %axis_index.21, s32[]{:T(128)} %bitcast.4, s32[1024]{0:T(1024)} %param.11, ...), kind=kLoop, calls=%fused_computation.128 | loop fusion | flops 133120 | bytes 28692 | tf_op jit(solution)/shard_map/sub | solution.py:52
  4.6 0.2 convert_reduce_fusion.2
  4.8 0.1 sub.173
  4.9 0.1 fusion.69
  5.0 0.6 fusion.73
  5.6 0.1 fusion.67
  5.7 0.4 convert_reduce_fusion
  6.1 0.1 convert_reduce_fusion.3
  6.3 0.1 sub.151
  6.4 0.1 fusion.65
  6.5 0.7 fusion.75
  7.2 0.1 select_reduce_fusion.7
  7.3 0.4 convert_reduce_fusion.1
  7.7 0.6 fusion.72
  8.3 0.1 fusion.68
  8.4 0.1 select_reduce_fusion.4
  8.5 0.1 convert_reduce_fusion.4.refs_1_
  8.7 0.4 select_reduce_fusion.2
  9.1 0.6 fusion.74
  9.7 0.1 select_reduce_fusion.6
  9.8 0.1 select_reduce_fusion.5
  9.9 0.1 convert_reduce_fusion.5.refs_1_
  10.0 0.1 select_reduce_fusion.3
  10.1 1.2 %select_reduce_fusion = s32[2176]{0:T(1024)S(1)} fusion(s32[1024]{0:T(1024)S(1)} %get-tuple-element.31, s32[1024]{0:T(1024)S(1)} %add_select_fusion.16), kind=kLoop, calls=%fused_computation | loop fusion | flops 6682496 | bytes 16896 | tf_op jit(solution)/shard_map/reduce_sum | solution.py:50
  11.4 0.7 %fusion.63 = s32[1024]{0:T(1024)S(1)} fusion(s32[1024]{0:T(1024)} %param.12, s32[1024]{0:T(1024)} %param.10, s32[]{:T(128)} %axis_index.23, s32[]{:T(128)S(6)} %axis_index.26), kind=kLoop, calls=%fused_computation.148 | loop fusion | flops 64512 | bytes 12296 | tf_op jit(solution)/shard_map/sub | solution.py:52
  13.3 1.4 %add_add_fusion.refs_0_ = s32[3]{0:T(128)S(1)} fusion(s32[1]{0:T(128)} %get-tuple-element.47, s32[1]{0:T(128)} %get-tuple-element.43, s32[1]{0:T(128)} %bitcast.1), kind=kLoop, calls=%fused_computation.195 | loop fusion | flops 6 | bytes 24 | tf_op jit(solution)/shard_map/stack | solution.py:200
  14.7 0.8 %add_add_fusion.1.refs_0_ = s32[3]{0:T(128)S(1)} fusion(s32[1]{0:T(128)S(6)} %add.272, s32[1]{0:T(128)} %get-tuple-element.42, s32[1]{0:T(128)} %bitcast.1), kind=kLoop, calls=%fused_computation.196 | loop fusion | flops 6 | bytes 24 | tf_op jit(solution)/shard_map/stack | solution.py:200
  15.4 0.0 collective-permute-done.refs_9_
  15.4 1.3 %collective-permute-start.1 = (f32[16,4096]{1,0:T(8,128)S(1)}, f32[16,4096]{1,0:T(8,128)S(1)}, u32[]{:S(2)}, u32[]{:S(2)}) collective-permute-start(f32[16,4096]{1,0:T(8,128)S(1)} %collective-permute-done.refs_9_), channel_id=1, source_target_pairs={{0,4},{4,8},{8,12},{12,0},{1,5},{5,9},{9,13},{13,1},{2,6},{6,10},{... | collective-permute-start | bytes 786440 | tf_op jit(solution)/shard_map/ppermute | solution.py:18
  16.8 1.0 %select_reduce_fusion.1 = s32[1792]{0:T(1024)S(1)} fusion(s32[1024]{0:T(1024)S(1)} %fusion.63, s32[1024]{0:T(1024)S(1)} %add_select_fusion.17), kind=kLoop, calls=%fused_computation.2 | loop fusion | flops 5503232 | bytes 15360 | tf_op jit(solution)/shard_map/reduce_sum | solution.py:50
  17.8 0.0 collective-permute-done.4.refs_6_
  17.8 0.6 collective-permute-start.5
  18.4 6.5 %collective-permute-done.1.refs_4_ = f32[16,4096]{1,0:T(8,128)S(1)} collective-permute-done((f32[16,4096]{1,0:T(8,128)S(1)}, f32[16,4096]{1,0:T(8,128)S(1)}, u32[]{:S(2)}, u32[]{:S(2)}) %collective-permute-start.1) | collective-permute-done | bytes 262176 | tf_op jit(solution)/shard_map/ppermute | solution.py:18
  24.9 0.0 collective-permute-start.2
  24.9 1.2 %add_add_fusion.2.refs_0_ = s32[3]{0:T(128)S(1)} fusion(s32[1]{0:T(128)} %get-tuple-element.44, s32[1]{0:T(128)} %get-tuple-element.41, s32[1]{0:T(128)} %bitcast.1), kind=kLoop, calls=%fused_computation.197 | loop fusion | flops 6 | bytes 24 | tf_op jit(solution)/shard_map/stack | solution.py:200
  26.2 0.0 collective-permute-done.3.refs_5_
  26.2 0.0 collective-permute-done.5.refs_7_
  26.2 0.0 copy-start
  26.2 0.9 %copy-done = f32[16,4096]{1,0:T(8,128)S(1)} copy-done((f32[16,4096]{1,0:T(8,128)S(1)}, f32[16,4096]{1,0:T(8,128)}, u32[]{:S(2)}) %copy-start) | copy-done | bytes 262168
  27.1 4.8 %shard_map.91 = (f32[1056,128]{1,0:T(8,128)S(1)}, bf16[2048,256]{1,0:T(8,128)(2,1)S(1)}, bf16[32,2,128,128]{3,2,1,0:T(8,128)(2,1)S(1)}) custom-call(s32[3]{0:T(128)S(1)} %add_add_fusion.1.refs_0_, s32[224]{0:T(256)S(1)} %convert_reduce_fusion.5.refs_1_, s32[1792]{0:T(1024)S(1)} %get-tuple-element.30.refs_2_, s32[1792]{0:T(1024)S(1)} %get-tuple-element.29.refs_3_, ...), custom_call_target="tpu_custom_call" | custom-call | tf_op jit(solution)/shard_map/pallas_call | solution.py:226
  31.9 2.5 %shard_map.92 = (f32[1056,128]{1,0:T(8,128)S(1)}, bf16[16,2,128,128]{3,2,1,0:T(8,128)(2,1)S(1)}) custom-call(s32[3]{0:T(128)S(1)} %add_add_fusion.2.refs_0_, s32[224]{0:T(256)S(1)} %convert_reduce_fusion.5.refs_1_, s32[1792]{0:T(1024)S(1)} %get-tuple-element.30.refs_2_, s32[1792]{0:T(1024)S(1)} %get-tuple-element.29.refs_3_, ...), custom_call_target="tpu_custom_call" | custom-call | tf_op jit(solution)/shard_map/pallas_call | solution.py:226
  34.4 0.0 collective-permute-done.2.refs_4_
  34.4 2.7 %shard_map.93 = (f32[16,4096]{1,0:T(8,128)S(1)}, f32[16,4096]{1,0:T(8,128)S(1)}, bf16[16,2,128,128]{3,2,1,0:T(8,128)(2,1)S(1)}) custom-call(s32[3]{0:T(128)S(1)} %add_add_fusion.refs_0_, s32[224]{0:T(256)S(1)} %convert_reduce_fusion.5.refs_1_, s32[1792]{0:T(1024)S(1)} %get-tuple-element.30.refs_2_, s32[1792]{0:T(1024)S(1)} %get-tuple-element.29.refs_3_, ...), custom_call_target="tpu_custom_call" | custom-call | tf_op jit(solution)/shard_map/pallas_call | solution.py:226
  37.1 7.5 %collective-permute-start.6 = (f32[16,4096]{1,0:T(8,128)S(1)}, f32[16,4096]{1,0:T(8,128)S(1)}, u32[]{:S(2)}, u32[]{:S(2)}) collective-permute-start(f32[16,4096]{1,0:T(8,128)S(1)} %get-tuple-element.20), channel_id=1, source_target_pairs={{0,1},{1,0},{2,3},{3,2},{4,5},{5,4},{6,7},{7,6},{8,9},{9,8},{10,11... | collective-permute-start | bytes 786440 | tf_op jit(solution)/shard_map/ppermute | solution.py:18
  44.6 1.3 %add_add_fusion.3.refs_0_ = s32[3]{0:T(128)S(1)} fusion(s32[1]{0:T(128)} %get-tuple-element.40, s32[1]{0:T(128)} %get-tuple-element.38, s32[1]{0:T(128)} %bitcast.1), kind=kLoop, calls=%fused_computation.198 | loop fusion | flops 6 | bytes 24 | tf_op jit(solution)/shard_map/stack | solution.py:200
  45.9 0.0 collective-permute-done.6
  45.9 1.3 %collective-permute-start.7 = (f32[16,4096]{1,0:T(8,128)S(1)}, f32[16,4096]{1,0:T(8,128)S(1)}, u32[]{:S(2)}, u32[]{:S(2)}) collective-permute-start(f32[16,4096]{1,0:T(8,128)S(1)} %add.273.refs_4_), channel_id=1, source_target_pairs={{0,2},{2,0},{1,3},{3,1},{4,6},{6,4},{5,7},{7,5},{8,10},{10,8},{9,1... | collective-permute-start | bytes 786440 | tf_op jit(solution)/shard_map/ppermute | solution.py:18
  47.2 1.4 %add_add_fusion.4.refs_0_ = s32[3]{0:T(128)S(1)} fusion(s32[1]{0:T(128)} %get-tuple-element.39, s32[1]{0:T(128)} %get-tuple-element.37, s32[1]{0:T(128)} %bitcast.1), kind=kLoop, calls=%fused_computation.199 | loop fusion | flops 6 | bytes 24 | tf_op jit(solution)/shard_map/stack | solution.py:200
  48.6 0.2 constant_dynamic-update-slice_fusion.2
  48.9 0.6 collective-permute-start.9
  49.4 4.2 %collective-permute-done.7.refs_4_ = f32[16,4096]{1,0:T(8,128)S(1)} collective-permute-done((f32[16,4096]{1,0:T(8,128)S(1)}, f32[16,4096]{1,0:T(8,128)S(1)}, u32[]{:S(2)}, u32[]{:S(2)}) %collective-permute-start.7) | collective-permute-done | bytes 262176 | tf_op jit(solution)/shard_map/ppermute | solution.py:18
  53.7 1.0 %collective-permute-start.8 = (f32[16,4096]{1,0:T(8,128)S(1)}, f32[16,4096]{1,0:T(8,128)S(1)}, u32[]{:S(2)}, u32[]{:S(2)}) collective-permute-start(f32[16,4096]{1,0:T(8,128)S(1)} %collective-permute-done.7.refs_4_), channel_id=1, source_target_pairs={{0,1},{1,0},{2,3},{3,2},{4,5},{5,4},{6,7},{7,6},{8,9},{9,8},{10,11... | collective-permute-start | bytes 786440 | tf_op jit(solution)/shard_map/ppermute | solution.py:18
  54.7 0.1 constant_dynamic-update-slice_fusion.1
  54.9 0.1 constant_dynamic-update-slice_fusion.refs_6_
  55.0 0.0 collective-permute-done.9.refs_5_
  55.0 7.8 %shard_map.94 = (f32[1056,128]{1,0:T(8,128)S(1)}, bf16[1024,256]{1,0:T(8,128)(2,1)}) custom-call(s32[3]{0:T(128)S(1)} %add_add_fusion.4.refs_0_, s32[272]{0:T(512)S(1)} %convert_reduce_fusion.4.refs_1_, s32[2176]{0:T(1024)S(1)} %get-tuple-element.28.refs_2_, s32[2176]{0:T(1024)S(1)} %get-tuple-element.27.refs_3_, f32[16,4096]{1,0:T(8,128)S(1)} %add.273.refs_4_, ...), custom_call_target="tpu_custom_call" | custom-call | tf_op jit(solution)/shard_map/pallas_call | solution.py:226
  62.8 0.0 collective-permute-done.8.refs_5_
  62.9 8.1 %shard_map.95 = (f32[16,4096]{1,0:T(8,128)S(1)}, f32[16,4096]{1,0:T(8,128)S(1)}, bf16[1024,256]{1,0:T(8,128)(2,1)}) custom-call(s32[3]{0:T(128)S(1)} %add_add_fusion.3.refs_0_, s32[272]{0:T(512)S(1)} %convert_reduce_fusion.4.refs_1_, s32[2176]{0:T(1024)S(1)} %get-tuple-element.28.refs_2_, s32[2176]{0:T(1024)S(1)} %get-tuple-element.27.refs_3_, ...), custom_call_target="tpu_custom_call" | custom-call | tf_op jit(solution)/shard_map/pallas_call | solution.py:226
  70.9 0.0 collective-permute-start.10
  70.9 1.5 %collective-permute-done.10 = f32[16,4096]{1,0:T(8,128)S(1)} collective-permute-done((f32[16,4096]{1,0:T(8,128)S(1)}, f32[16,4096]{1,0:T(8,128)S(1)}, u32[]{:S(2)}, u32[]{:S(2)}) %collective-permute-start.10) | collective-permute-done | bytes 262176 | tf_op jit(solution)/shard_map/ppermute | solution.py:18
  72.5 0.7 %multiply_subtract_fusion = f32[16,4096]{1,0:T(8,128)} fusion(f32[16,4096]{1,0:T(8,128)S(1)} %get-tuple-element.25, f32[16,4096]{1,0:T(8,128)S(1)} %collective-permute-done.10, f32[16,4096]{1,0:T(8,128)S(1)} %add.273.refs_4_), kind=kLoop, calls=%fused_computation.12 | loop fusion | flops 262144 | bytes 1048576 | tf_op jit(solution)/shard_map/sub | solution.py:306
  (13 shorter events, 0.1 us)
Async XLA Ops:
  0.0 15.4 %collective-permute-start = (f32[16,4096]{1,0:T(8,128)}, f32[16,4096]{1,0:T(8,128)S(1)}, u32[]{:S(2)}, u32[]{:S(2)}) collective-permute-start(f32[16,4096]{1,0:T(8,128)} %refs_8_.1), channel_id=1, source_target_pairs={{0,4},{4,8},{8,12},{12,0},{1,5},{5,9},{9,13},{13,1},{2,6},{6,10},{... | collective-permute-start | bytes 786440 | tf_op jit(solution)/shard_map/ppermute | solution.py:18
  1.3 24.9 %collective-permute-start.3 = (f32[16,4096]{1,0:T(8,128)}, f32[16,4096]{1,0:T(8,128)S(1)}, u32[]{:S(2)}, u32[]{:S(2)}) collective-permute-start(f32[16,4096]{1,0:T(8,128)} %refs_8_.1), channel_id=1, source_target_pairs={{0,1},{1,0},{2,3},{3,2},{4,5},{5,4},{6,7},{7,6},{8,9},{9,8},{10,11... | collective-permute-start | bytes 786440 | tf_op jit(solution)/shard_map/ppermute | solution.py:18
  2.3 15.5 %collective-permute-start.4 = (f32[16,4096]{1,0:T(8,128)}, f32[16,4096]{1,0:T(8,128)S(1)}, u32[]{:S(2)}, u32[]{:S(2)}) collective-permute-start(f32[16,4096]{1,0:T(8,128)} %refs_8_.1), channel_id=1, source_target_pairs={{0,2},{2,0},{1,3},{3,1},{4,6},{6,4},{5,7},{7,5},{8,10},{10,8},{9,1... | collective-permute-start | bytes 786440 | tf_op jit(solution)/shard_map/ppermute | solution.py:18
  15.4 9.5 %collective-permute-start.1 = (f32[16,4096]{1,0:T(8,128)S(1)}, f32[16,4096]{1,0:T(8,128)S(1)}, u32[]{:S(2)}, u32[]{:S(2)}) collective-permute-start(f32[16,4096]{1,0:T(8,128)S(1)} %collective-permute-done.refs_9_), channel_id=1, source_target_pairs={{0,4},{4,8},{8,12},{12,0},{1,5},{5,9},{9,13},{13,1},{2,6},{6,10},{... | collective-permute-start | bytes 786440 | tf_op jit(solution)/shard_map/ppermute | solution.py:18
  17.8 8.4 %collective-permute-start.5 = (f32[16,4096]{1,0:T(8,128)S(1)}, f32[16,4096]{1,0:T(8,128)S(1)}, u32[]{:S(2)}, u32[]{:S(2)}) collective-permute-start(f32[16,4096]{1,0:T(8,128)S(1)} %collective-permute-done.4.refs_6_), channel_id=1, source_target_pairs={{0,1},{1,0},{2,3},{3,2},{4,5},{5,4},{6,7},{7,6},{8,9},{9,8},{10,11... | collective-permute-start | bytes 786440 | tf_op jit(solution)/shard_map/ppermute | solution.py:18
  24.9 9.5 %collective-permute-start.2 = (f32[16,4096]{1,0:T(8,128)S(1)}, f32[16,4096]{1,0:T(8,128)S(1)}, u32[]{:S(2)}, u32[]{:S(2)}) collective-permute-start(f32[16,4096]{1,0:T(8,128)S(1)} %collective-permute-done.1.refs_4_), channel_id=1, source_target_pairs={{0,4},{4,8},{8,12},{12,0},{1,5},{5,9},{9,13},{13,1},{2,6},{6,10},{... | collective-permute-start | bytes 786440 | tf_op jit(solution)/shard_map/ppermute | solution.py:18
  26.2 1.0 %copy-start = (f32[16,4096]{1,0:T(8,128)S(1)}, f32[16,4096]{1,0:T(8,128)}, u32[]{:S(2)}) copy-start(f32[16,4096]{1,0:T(8,128)} %refs_8_.1) | copy-start | bytes 786436
  37.1 8.7 %collective-permute-start.6 = (f32[16,4096]{1,0:T(8,128)S(1)}, f32[16,4096]{1,0:T(8,128)S(1)}, u32[]{:S(2)}, u32[]{:S(2)}) collective-permute-start(f32[16,4096]{1,0:T(8,128)S(1)} %get-tuple-element.20), channel_id=1, source_target_pairs={{0,1},{1,0},{2,3},{3,2},{4,5},{5,4},{6,7},{7,6},{8,9},{9,8},{10,11... | collective-permute-start | bytes 786440 | tf_op jit(solution)/shard_map/ppermute | solution.py:18
  45.9 7.7 %collective-permute-start.7 = (f32[16,4096]{1,0:T(8,128)S(1)}, f32[16,4096]{1,0:T(8,128)S(1)}, u32[]{:S(2)}, u32[]{:S(2)}) collective-permute-start(f32[16,4096]{1,0:T(8,128)S(1)} %add.273.refs_4_), channel_id=1, source_target_pairs={{0,2},{2,0},{1,3},{3,1},{4,6},{6,4},{5,7},{7,5},{8,10},{10,8},{9,1... | collective-permute-start | bytes 786440 | tf_op jit(solution)/shard_map/ppermute | solution.py:18
  48.9 6.2 %collective-permute-start.9 = (f32[16,4096]{1,0:T(8,128)S(1)}, f32[16,4096]{1,0:T(8,128)S(1)}, u32[]{:S(2)}, u32[]{:S(2)}) collective-permute-start(f32[16,4096]{1,0:T(8,128)S(1)} %add.273.refs_4_), channel_id=1, source_target_pairs={{0,1},{1,0},{2,3},{3,2},{4,5},{5,4},{6,7},{7,6},{8,9},{9,8},{10,11... | collective-permute-start | bytes 786440 | tf_op jit(solution)/shard_map/ppermute | solution.py:18
  53.7 9.2 %collective-permute-start.8 = (f32[16,4096]{1,0:T(8,128)S(1)}, f32[16,4096]{1,0:T(8,128)S(1)}, u32[]{:S(2)}, u32[]{:S(2)}) collective-permute-start(f32[16,4096]{1,0:T(8,128)S(1)} %collective-permute-done.7.refs_4_), channel_id=1, source_target_pairs={{0,1},{1,0},{2,3},{3,2},{4,5},{5,4},{6,7},{7,6},{8,9},{9,8},{10,11... | collective-permute-start | bytes 786440 | tf_op jit(solution)/shard_map/ppermute | solution.py:18
  70.9 1.5 %collective-permute-start.10 = (f32[16,4096]{1,0:T(8,128)S(1)}, f32[16,4096]{1,0:T(8,128)S(1)}, u32[]{:S(2)}, u32[]{:S(2)}) collective-permute-start(f32[16,4096]{1,0:T(8,128)S(1)} %get-tuple-element.26), channel_id=1, source_target_pairs={{0,1},{1,0},{2,3},{3,2},{4,5},{5,4},{6,7},{7,6},{8,9},{9,8},{10,11... | collective-permute-start | bytes 786440 | tf_op jit(solution)/shard_map/ppermute | solution.py:18

commit v2 on v1

--- a/solution.py
+++ b/solution.py
@@ -64,10 +64,10 @@
     )
 
 
-def kernel(raw_lefts, raw_rights, has_left, has_right, has_sum, last, slots, first_group, refs):
+def kernel(raw_lefts, raw_rights, has_left, has_right, has_sum, last, slots, first_group, segs, refs):
     refs = list(refs)
-    meta, rights, lefts, outs = refs[:4]
-    refs = refs[4:]
+    first, turn_count, rights, lefts, outs = refs[:5]
+    refs = refs[5:]
     left_raw, refs = refs[:raw_lefts], refs[raw_lefts:]
     right_raw, refs = refs[:raw_rights], refs[raw_rights:]
     panel, given, sum_in = None, [], None
@@ -152,7 +152,9 @@
             sums[unit][rows, :] += product[task * 32 : task * 32 + 32]
 
     def work(*totals):
-        begin, turns = meta[0] * TURN, meta[1]
+        begin, turns = first[segs[0]] * TURN, turn_count[segs[0]]
+        for seg in segs[1:]:
+            turns = turns + turn_count[seg]
         for unit in range(2):
             issue(begin + unit, unit, totals[unit])
 
@@ -180,7 +182,7 @@
         results[0][...] = sum_0[...] + sum_1[...]
         return
     sum_0[...] = sum_0[...] + sum_1[...]
-    layer = meta[2]
+    layer = lax.axis_index("depth")
     size = results[0].shape[0]
     layers = slots // size
     for index, result in enumerate(results):
@@ -194,14 +196,11 @@
 
 def tile_sum(tasks, seg, seg_count, left_raw, right_raw, panel, given, sum_in, last, slots, width, first_group):
     f32, bf16 = jnp.float32, jnp.bfloat16
-    turns = tasks["turns"][seg]
-    for other in range(seg + 1, seg + seg_count):
-        turns = turns + tasks["turns"][other]
-    meta = jnp.stack([tasks["first"][seg], turns, lax.axis_index("depth")]).astype(jnp.int32)
-    args = [meta, tasks["rights"], tasks["left"], tasks["out"], *left_raw, *right_raw]
+    plans = [tasks[name] for name in ("first", "turns", "rights", "left", "out")]
+    args = [*plans, *left_raw, *right_raw]
     smem, vmem = pl.BlockSpec(memory_space=pltpu.SMEM), pl.BlockSpec(memory_space=pltpu.VMEM)
     extra = [v for v in [panel, *given, sum_in] if v is not None]
-    in_specs = [smem] * 4 + [vmem] * (len(left_raw) + len(right_raw) + len(extra))
+    in_specs = [smem] * 5 + [vmem] * (len(left_raw) + len(right_raw) + len(extra))
     sum_shape = ((slots + 1) * 32, 128)
     shapes = (
         [jax.ShapeDtypeStruct((OUT_DEV, width), f32)] * 2
@@ -222,6 +221,7 @@
         last,
         slots,
         first_group,
+        tuple(range(seg, seg + seg_count)),
     )
     return pl.pallas_call(
         lambda *refs: body(refs),
@@ -273,6 +273,9 @@
     key = jnp.where(place < square_count[0], moved_right(square_right), groups)
     chunks = -(-(tasks // CHUNK + groups + TURN * rows + TURN) // 16) * 16
     square_tasks = plan(key, left, square_out, groups, per_dev, slots, chunks)
+    cube_left, cube_right, cube_out, cube_count, _ = lax.optimization_barrier(
+        (cube_left, cube_right, cube_out, cube_count, column[1])
+    )
     from_col, left = moved_left(cube_left)
     left = left - jnp.where(from_col == 0, 0, layers * per_dev)
     key = jnp.where(from_col == 0, 0, groups) + moved_right(cube_right)
@@ -295,12 +298,15 @@
     weights = jnp.concatenate(weights, axis=0)
     square = mine + ring(other, "depth")
 
-    squares = [piece for value in ring_all(square, "col") for piece in ring_all(value, "depth")]
-    total, near = tile_sum(
-        cube_tasks, 0, 1, squares[:layers], [], None, [weights], None, False, slots, width, 0
-    )
+    near = ring_all(square, "depth")
+    far = ring_all(square, "col")[1:]
+    total, _ = tile_sum(
+        cube_tasks, 0, 1, near, [], None, [weights], None, False, slots, width, 0
+    )
+    total, *far = lax.optimization_barrier((total, *far))
+    far = [piece for value in far for piece in ring_all(value, "depth")]
     mine, other, _ = tile_sum(
-        cube_tasks, 1, 1, squares[layers:], [], None, [weights], total, True, slots, width, groups
+        cube_tasks, 1, 1, far, [], None, [weights], total, True, slots, width, groups
     )
     cube = mine + ring(other, "depth")
     return 3.0 * square - 2.0 * cube

time: 73.5 us -> 63.4 us (0.86)
  the two profiles are of different devices: /device:TPU:3 before, /device:TPU:0 now
where the time goes in v2:
time: 63.4 us; the launch traced here: 63.5 us
  Pallas kernels  31.6 us (50%)
  waiting for transfers between devices  14.8 us (23%)
  other arithmetic  8.03 us (13%)
  starting transfers between devices  5.94 us (9%)
  local copies, waits for them, and re-layouts  1.62 us (3%)
  between operations  1.5 us (2%)
    pallas_call x5, Pallas kernels, tile_sum(): pl.pallas_call(lambda *refs: body(refs), out_shape=shapes, in_specs=in_sp...  31.6 us
    ppermute x11, waiting for transfers between devices, ring(): return lax.ppermute(value, axis, [(i, (i + 1) % size) for i in range(size)])  14.8 us
    ppermute x11, starting transfers between devices, ring(): return lax.ppermute(value, axis, [(i, (i + 1) % size) for i in range(size)])  5.94 us
    reduce_sum x2, other arithmetic, plan(): jnp.sum(jnp.where(position[:, None] == slot[None, :], (left * (slots + 1)...  2.24 us
    unnamed x4, local copies, waits for them, and re-layouts  1.32 us
  transfers between devices with their start and end apart: 11, of which 6 were waited for; matrix products, arithmetic and copies ran while one was open for 12% of the time, Pallas kernels for 31%

profile of v2, /device:TPU:0, one launch (start us, length us, event | category | flops | bytes accessed | tf_op | source)
XLA Modules:
  0.0 63.5 jit_solution(16328047450666160148)
XLA Ops:
  0.0 3.0 %collective-permute-start = (f32[16,4096]{1,0:T(8,128)}, f32[16,4096]{1,0:T(8,128)S(1)}, u32[]{:S(2)}, u32[]{:S(2)}) collective-permute-start(f32[16,4096]{1,0:T(8,128)} %refs_9_.1), channel_id=1, source_target_pairs={{0,4},{4,8},{8,12},{12,0},{1,5},{5,9},{9,13},{13,1},{2,6},{6,10},{... | collective-permute-start | bytes 786440 | tf_op jit(solution)/shard_map/ppermute | solution.py:18
  3.0 0.0 collective-permute-start.3
  3.0 1.5 %collective-permute-start.4 = (f32[16,4096]{1,0:T(8,128)}, f32[16,4096]{1,0:T(8,128)S(1)}, u32[]{:S(2)}, u32[]{:S(2)}) collective-permute-start(f32[16,4096]{1,0:T(8,128)} %refs_9_.1), channel_id=1, source_target_pairs={{0,2},{2,0},{1,3},{3,1},{4,6},{6,4},{5,7},{7,5},{8,10},{10,8},{9,1... | collective-permute-start | bytes 786440 | tf_op jit(solution)/shard_map/ppermute | solution.py:18
  5.2 0.7 %fusion.15 = s32[1024]{0:T(1024)S(1)} fusion(s32[1024]{0:T(1024)} %param.11, s32[]{:T(128)S(6)} %axis_index.33, s32[]{:T(128)} %bitcast.2), kind=kLoop, calls=%fused_computation.92 | loop fusion | flops 31744 | bytes 8200 | tf_op jit(solution)/shard_map/jit(_where)/select_n | solution.py:273
  5.9 0.1 convert_reduce_fusion.3
  6.0 0.4 convert_reduce_fusion.1
  6.4 0.1 sub.151
  6.5 0.1 fusion.65
  6.7 0.1 select_reduce_fusion.7.refs_0_
  6.8 0.1 select_reduce_fusion.5
  6.9 0.1 select_reduce_fusion.6
  6.9 0.1 convert_reduce_fusion.5.refs_2_
  7.0 0.1 select_reduce_fusion.3
  7.8 0.7 %add_select_fusion.17 = s32[1024]{0:T(1024)S(1)} fusion(s32[1024]{0:T(1024)S(1)} %select_reduce_fusion.3, s32[1024]{0:T(1024)S(1)} %convert_reduce_fusion.1, s32[1024]{0:T(1024)} %param.11, s32[]{:T(128)S(6)} %axis_index.33, s32[]{:T(128)} %bitcast.3), kind=kLoop, calls=%fused_computation.136 | loop fusion | flops 34816 | bytes 16392 | tf_op jit(solution)/shard_map/jit(_where)/select_n | solution.py:48
  8.5 3.0 %collective-permute-done.refs_10_ = f32[16,4096]{1,0:T(8,128)S(1)} collective-permute-done((f32[16,4096]{1,0:T(8,128)}, f32[16,4096]{1,0:T(8,128)S(1)}, u32[]{:S(2)}, u32[]{:S(2)}) %collective-permute-start) | collective-permute-done | bytes 262176 | tf_op jit(solution)/shard_map/ppermute | solution.py:18
  11.6 0.8 %fusion.51 = (s32[1024]{0:T(1024)S(1)}, s32[1024]{0:T(1024)S(1)}, s32[1024]{0:T(1024)S(1)}) fusion(s32[1024]{0:T(1024)} %param.16, s32[1024]{0:T(1024)} %param.14, s32[]{:T(128)S(6)} %axis_index.38, s32[]{:T(128)S(6)} %axis_index.36, s32[1024]{0:T(1024)} %param.15, s32[]{:T(128)S(6)} %axis_index.33, s32[]{:T(128)} %bitcast.4, s32[1024]{0:T(1024)} %param.12, ...), kind=kLoop, calls=%fused_computation.128 | loop fusion | flops 165888 | bytes 32784 | tf_op jit(solution)/shard_map/sub | solution.py:52
  12.4 0.2 convert_reduce_fusion.2
  12.6 0.4 convert_reduce_fusion
  13.0 0.1 sub.173
  13.1 0.1 fusion.69
  13.2 0.1 fusion.67.refs_0_
  13.3 0.1 select_reduce_fusion.4
  13.4 0.1 fusion.68
  13.5 0.4 select_reduce_fusion.2
  13.9 0.1 collective-permute-start.1
  14.0 1.2 %select_reduce_fusion = s32[2176]{0:T(1024)S(1)} fusion(s32[1024]{0:T(1024)S(1)} %get-tuple-element.43, s32[1024]{0:T(1024)S(1)} %add_select_fusion.16), kind=kLoop, calls=%fused_computation | loop fusion | flops 6682496 | bytes 16896 | tf_op jit(solution)/shard_map/reduce_sum | solution.py:50
  15.2 0.0 collective-permute-done.4.refs_7_
  15.2 0.1 collective-permute-start.5
  15.3 1.0 %select_reduce_fusion.1 = s32[1792]{0:T(1024)S(1)} fusion(s32[1024]{0:T(1024)S(1)} %get-tuple-element.53, s32[1024]{0:T(1024)S(1)} %add_select_fusion.17), kind=kLoop, calls=%fused_computation.2 | loop fusion | flops 5503232 | bytes 15360 | tf_op jit(solution)/shard_map/reduce_sum | solution.py:50
  16.3 6.9 %collective-permute-done.1.refs_5_ = f32[16,4096]{1,0:T(8,128)S(1)} collective-permute-done((f32[16,4096]{1,0:T(8,128)S(1)}, f32[16,4096]{1,0:T(8,128)S(1)}, u32[]{:S(2)}, u32[]{:S(2)}) %collective-permute-start.1) | collective-permute-done | bytes 262176 | tf_op jit(solution)/shard_map/ppermute | solution.py:18
  23.2 0.0 collective-permute-start.2
  23.3 0.0 collective-permute-done.3.refs_6_
  23.3 0.0 collective-permute-done.5.refs_8_
  23.3 0.0 copy-start
  23.3 0.9 %copy-done = f32[16,4096]{1,0:T(8,128)S(1)} copy-done((f32[16,4096]{1,0:T(8,128)S(1)}, f32[16,4096]{1,0:T(8,128)}, u32[]{:S(2)}) %copy-start) | copy-done | bytes 262168
  24.3 8.1 %shard_map.91 = (f32[1056,128]{1,0:T(8,128)S(1)}, bf16[2048,256]{1,0:T(8,128)(2,1)S(1)}, bf16[32,2,128,128]{3,2,1,0:T(8,128)(2,1)S(1)}) custom-call(s32[4]{0:T(128)S(1)} %select_reduce_fusion.7.refs_0_, s32[4]{0:T(128)S(1)} %and_select_fusion.6.refs_1_, s32[224]{0:T(256)S(1)} %convert_reduce_fusion.5.refs_2_, s32[1792]{0:T(1024)S(1)} %get-tuple-element.42.refs_3_, ...), custom_call_target="tpu_custom_call" | custom-call | tf_op jit(solution)/shard_map/pallas_call | solution.py:226
  32.4 3.9 %shard_map.92 = (f32[1056,128]{1,0:T(8,128)S(1)}, bf16[16,2,128,128]{3,2,1,0:T(8,128)(2,1)S(1)}) custom-call(s32[4]{0:T(128)S(1)} %select_reduce_fusion.7.refs_0_, s32[4]{0:T(128)S(1)} %and_select_fusion.6.refs_1_, s32[224]{0:T(256)S(1)} %convert_reduce_fusion.5.refs_2_, s32[1792]{0:T(1024)S(1)} %get-tuple-element.42.refs_3_, ...), custom_call_target="tpu_custom_call" | custom-call | tf_op jit(solution)/shard_map/pallas_call | solution.py:226
  36.3 0.0 collective-permute-done.2.refs_5_
  36.3 4.2 %shard_map.93 = (f32[16,4096]{1,0:T(8,128)S(1)}, f32[16,4096]{1,0:T(8,128)S(1)}, bf16[16,2,128,128]{3,2,1,0:T(8,128)(2,1)S(1)}) custom-call(s32[4]{0:T(128)S(1)} %select_reduce_fusion.7.refs_0_, s32[4]{0:T(128)S(1)} %and_select_fusion.6.refs_1_, s32[224]{0:T(256)S(1)} %convert_reduce_fusion.5.refs_2_, s32[1792]{0:T(1024)S(1)} %get-tuple-element.42.refs_3_, ...), custom_call_target="tpu_custom_call" | custom-call | tf_op jit(solution)/shard_map/pallas_call | solution.py:226
  40.6 0.1 collective-permute-start.6
  40.7 0.1 convert_reduce_fusion.4.refs_2_
  40.8 0.2 constant_dynamic-update-slice_fusion.2
  41.1 1.1 %collective-permute-done.6 = f32[16,4096]{1,0:T(8,128)S(1)} collective-permute-done((f32[16,4096]{1,0:T(8,128)S(1)}, f32[16,4096]{1,0:T(8,128)S(1)}, u32[]{:S(2)}, u32[]{:S(2)}) %collective-permute-start.6) | collective-permute-done | bytes 262176 | tf_op jit(solution)/shard_map/ppermute | solution.py:18
  42.2 0.2 collective-permute-start.7
  42.4 0.0 collective-permute-start.8
  42.4 0.1 constant_dynamic-update-slice_fusion.1
  42.6 0.1 constant_dynamic-update-slice_fusion.refs_7_
  42.7 1.1 %collective-permute-done.7.refs_6_ = f32[16,4096]{1,0:T(8,128)S(1)} collective-permute-done((f32[16,4096]{1,0:T(8,128)S(1)}, f32[16,4096]{1,0:T(8,128)S(1)}, u32[]{:S(2)}, u32[]{:S(2)}) %collective-permute-start.7) | collective-permute-done | bytes 262176 | tf_op jit(solution)/shard_map/ppermute | solution.py:18
  43.8 7.4 %shard_map.94 = (f32[1056,128]{1,0:T(8,128)S(1)}, bf16[1024,256]{1,0:T(8,128)(2,1)}) custom-call(s32[2]{0:T(128)S(1)} %fusion.67.refs_0_, s32[2]{0:T(128)S(1)} %and_select_fusion.2.refs_1_, s32[272]{0:T(512)S(1)} %convert_reduce_fusion.4.refs_2_, s32[2176]{0:T(1024)S(1)} %get-tuple-element.40.refs_3_, s32[2176]{0:T(1024)S(1)} %get-tuple-element.39.refs_4_, ...), custom_call_target="tpu_custom_call" | custom-call | tf_op jit(solution)/shard_map/pallas_call | solution.py:226
  51.3 0.0 collective-permute-done.8.refs_5_
  51.3 0.9 %collective-permute-start.9 = (f32[16,4096]{1,0:T(8,128)S(1)}, f32[16,4096]{1,0:T(8,128)S(1)}, u32[]{:S(2)}, u32[]{:S(2)}) collective-permute-start(f32[16,4096]{1,0:T(8,128)S(1)} %collective-permute-done.8.refs_5_), channel_id=1, source_target_pairs={{0,1},{1,0},{2,3},{3,2},{4,5},{5,4},{6,7},{7,6},{8,9},{9,8},{10,11... | collective-permute-start | bytes 786440 | tf_op jit(solution)/shard_map/ppermute | solution.py:18
  52.2 1.2 %collective-permute-done.9.refs_6_ = f32[16,4096]{1,0:T(8,128)S(1)} collective-permute-done((f32[16,4096]{1,0:T(8,128)S(1)}, f32[16,4096]{1,0:T(8,128)S(1)}, u32[]{:S(2)}, u32[]{:S(2)}) %collective-permute-start.9) | collective-permute-done | bytes 262176 | tf_op jit(solution)/shard_map/ppermute | solution.py:18
  53.3 7.9 %shard_map.95 = (f32[16,4096]{1,0:T(8,128)S(1)}, f32[16,4096]{1,0:T(8,128)S(1)}, bf16[1024,256]{1,0:T(8,128)(2,1)}) custom-call(s32[2]{0:T(128)S(1)} %fusion.67.refs_0_, s32[2]{0:T(128)S(1)} %and_select_fusion.2.refs_1_, s32[272]{0:T(512)S(1)} %convert_reduce_fusion.4.refs_2_, s32[2176]{0:T(1024)S(1)} %get-tuple-element.40.refs_3_, ...), custom_call_target="tpu_custom_call" | custom-call | tf_op jit(solution)/shard_map/pallas_call | solution.py:226
  61.2 0.1 collective-permute-start.10
  61.3 1.4 %collective-permute-done.10 = f32[16,4096]{1,0:T(8,128)S(1)} collective-permute-done((f32[16,4096]{1,0:T(8,128)S(1)}, f32[16,4096]{1,0:T(8,128)S(1)}, u32[]{:S(2)}, u32[]{:S(2)}) %collective-permute-start.10) | collective-permute-done | bytes 262176 | tf_op jit(solution)/shard_map/ppermute | solution.py:18
  62.7 0.7 %multiply_subtract_fusion = f32[16,4096]{1,0:T(8,128)} fusion(f32[16,4096]{1,0:T(8,128)S(1)} %get-tuple-element.37, f32[16,4096]{1,0:T(8,128)S(1)} %collective-permute-done.10, f32[16,4096]{1,0:T(8,128)S(1)} %add.268.refs_5_), kind=kLoop, calls=%fused_computation.12 | loop fusion | flops 262144 | bytes 1048576 | tf_op jit(solution)/shard_map/sub | solution.py:312
  (11 shorter events, 0.1 us)
Async XLA Ops:
  0.0 11.6 %collective-permute-start = (f32[16,4096]{1,0:T(8,128)}, f32[16,4096]{1,0:T(8,128)S(1)}, u32[]{:S(2)}, u32[]{:S(2)}) collective-permute-start(f32[16,4096]{1,0:T(8,128)} %refs_9_.1), channel_id=1, source_target_pairs={{0,4},{4,8},{8,12},{12,0},{1,5},{5,9},{9,13},{13,1},{2,6},{6,10},{... | collective-permute-start | bytes 786440 | tf_op jit(solution)/shard_map/ppermute | solution.py:18
  3.0 20.3 %collective-permute-start.3 = (f32[16,4096]{1,0:T(8,128)}, f32[16,4096]{1,0:T(8,128)S(1)}, u32[]{:S(2)}, u32[]{:S(2)}) collective-permute-start(f32[16,4096]{1,0:T(8,128)} %refs_9_.1), channel_id=1, source_target_pairs={{0,1},{1,0},{2,3},{3,2},{4,5},{5,4},{6,7},{7,6},{8,9},{9,8},{10,11... | collective-permute-start | bytes 786440 | tf_op jit(solution)/shard_map/ppermute | solution.py:18
  3.0 12.2 %collective-permute-start.4 = (f32[16,4096]{1,0:T(8,128)}, f32[16,4096]{1,0:T(8,128)S(1)}, u32[]{:S(2)}, u32[]{:S(2)}) collective-permute-start(f32[16,4096]{1,0:T(8,128)} %refs_9_.1), channel_id=1, source_target_pairs={{0,2},{2,0},{1,3},{3,1},{4,6},{6,4},{5,7},{7,5},{8,10},{10,8},{9,1... | collective-permute-start | bytes 786440 | tf_op jit(solution)/shard_map/ppermute | solution.py:18
  13.9 9.3 %collective-permute-start.1 = (f32[16,4096]{1,0:T(8,128)S(1)}, f32[16,4096]{1,0:T(8,128)S(1)}, u32[]{:S(2)}, u32[]{:S(2)}) collective-permute-start(f32[16,4096]{1,0:T(8,128)S(1)} %collective-permute-done.refs_10_), channel_id=1, source_target_pairs={{0,4},{4,8},{8,12},{12,0},{1,5},{5,9},{9,13},{13,1},{2,6},{6,10},{... | collective-permute-start | bytes 786440 | tf_op jit(solution)/shard_map/ppermute | solution.py:18
  15.2 8.1 %collective-permute-start.5 = (f32[16,4096]{1,0:T(8,128)S(1)}, f32[16,4096]{1,0:T(8,128)S(1)}, u32[]{:S(2)}, u32[]{:S(2)}) collective-permute-start(f32[16,4096]{1,0:T(8,128)S(1)} %collective-permute-done.4.refs_7_), channel_id=1, source_target_pairs={{0,1},{1,0},{2,3},{3,2},{4,5},{5,4},{6,7},{7,6},{8,9},{9,8},{10,11... | collective-permute-start | bytes 786440 | tf_op jit(solution)/shard_map/ppermute | solution.py:18
  23.2 13.1 %collective-permute-start.2 = (f32[16,4096]{1,0:T(8,128)S(1)}, f32[16,4096]{1,0:T(8,128)S(1)}, u32[]{:S(2)}, u32[]{:S(2)}) collective-permute-start(f32[16,4096]{1,0:T(8,128)S(1)} %collective-permute-done.1.refs_5_), channel_id=1, source_target_pairs={{0,4},{4,8},{8,12},{12,0},{1,5},{5,9},{9,13},{13,1},{2,6},{6,10},{... | collective-permute-start | bytes 786440 | tf_op jit(solution)/shard_map/ppermute | solution.py:18
  23.3 1.0 %copy-start = (f32[16,4096]{1,0:T(8,128)S(1)}, f32[16,4096]{1,0:T(8,128)}, u32[]{:S(2)}) copy-start(f32[16,4096]{1,0:T(8,128)} %refs_9_.1) | copy-start | bytes 786436
  40.6 1.6 %collective-permute-start.6 = (f32[16,4096]{1,0:T(8,128)S(1)}, f32[16,4096]{1,0:T(8,128)S(1)}, u32[]{:S(2)}, u32[]{:S(2)}) collective-permute-start(f32[16,4096]{1,0:T(8,128)S(1)} %get-tuple-element.26), channel_id=1, source_target_pairs={{0,1},{1,0},{2,3},{3,2},{4,5},{5,4},{6,7},{7,6},{8,9},{9,8},{10,11... | collective-permute-start | bytes 786440 | tf_op jit(solution)/shard_map/ppermute | solution.py:18
  42.2 1.6 %collective-permute-start.7 = (f32[16,4096]{1,0:T(8,128)S(1)}, f32[16,4096]{1,0:T(8,128)S(1)}, u32[]{:S(2)}, u32[]{:S(2)}) collective-permute-start(f32[16,4096]{1,0:T(8,128)S(1)} %add.268.refs_5_), channel_id=1, source_target_pairs={{0,1},{1,0},{2,3},{3,2},{4,5},{5,4},{6,7},{7,6},{8,9},{9,8},{10,11... | collective-permute-start | bytes 786440 | tf_op jit(solution)/shard_map/ppermute | solution.py:18
  42.4 8.9 %collective-permute-start.8 = (f32[16,4096]{1,0:T(8,128)S(1)}, f32[16,4096]{1,0:T(8,128)S(1)}, u32[]{:S(2)}, u32[]{:S(2)}) collective-permute-start(f32[16,4096]{1,0:T(8,128)S(1)} %add.268.refs_5_), channel_id=1, source_target_pairs={{0,2},{2,0},{1,3},{3,1},{4,6},{6,4},{5,7},{7,5},{8,10},{10,8},{9,1... | collective-permute-start | bytes 786440 | tf_op jit(solution)/shard_map/ppermute | solution.py:18
  51.3 2.1 %collective-permute-start.9 = (f32[16,4096]{1,0:T(8,128)S(1)}, f32[16,4096]{1,0:T(8,128)S(1)}, u32[]{:S(2)}, u32[]{:S(2)}) collective-permute-start(f32[16,4096]{1,0:T(8,128)S(1)} %collective-permute-done.8.refs_5_), channel_id=1, source_target_pairs={{0,1},{1,0},{2,3},{3,2},{4,5},{5,4},{6,7},{7,6},{8,9},{9,8},{10,11... | collective-permute-start | bytes 786440 | tf_op jit(solution)/shard_map/ppermute | solution.py:18
  61.2 1.5 %collective-permute-start.10 = (f32[16,4096]{1,0:T(8,128)S(1)}, f32[16,4096]{1,0:T(8,128)S(1)}, u32[]{:S(2)}, u32[]{:S(2)}) collective-permute-start(f32[16,4096]{1,0:T(8,128)S(1)} %get-tuple-element.38), channel_id=1, source_target_pairs={{0,1},{1,0},{2,3},{3,2},{4,5},{5,4},{6,7},{7,6},{8,9},{9,8},{10,11... | collective-permute-start | bytes 786440 | tf_op jit(solution)/shard_map/ppermute | solution.py:18

commit v3 on v2

--- a/solution.py
+++ b/solution.py
@@ -13,9 +13,9 @@
 TURN = 4
 
 
-def ring(value, axis):
+def ring(value, axis, step=1):
     size = lax.axis_size(axis)
-    return lax.ppermute(value, axis, [(i, (i + 1) % size) for i in range(size)])
+    return lax.ppermute(value, axis, [(i, (i + step) % size) for i in range(size)])
 
 
 def ring_all(value, axis):
@@ -262,10 +262,19 @@
         return from_col, (from_col * layers + from_layer) * per_dev + left % per_dev
 
     def moved_right(right):
-        return lax.rem(row - right // per_dev + rows, rows) * per_dev + right % per_dev
-
-    column = ring_all(density, "row")
+        away = lax.rem(row - right // per_dev + rows, rows)
+        order = jnp.where(
+            2 * away <= rows - 1 + rows % 2, 2 * away - 1, jnp.minimum(2 * (rows - away), rows - 1)
+        )
+        return jnp.maximum(order, 0) * per_dev + right % per_dev
+
+    column = [density]
+    for _ in range((rows - 1) // 2):
+        ahead, behind = (column[-2], column[-1]) if len(column) > 1 else (density, density)
+        column += [ring(ahead, "row"), ring(behind, "row", -1)]
     across = ring_all(density, "col")
+    if rows % 2 == 0:
+        opposite = ring(column[-2] if rows > 2 else density, "row")
     lefts = [piece for value in across for piece in ring_all(value, "depth")]
 
     groups = rows * per_dev
@@ -273,9 +282,6 @@
     key = jnp.where(place < square_count[0], moved_right(square_right), groups)
     chunks = -(-(tasks // CHUNK + groups + TURN * rows + TURN) // 16) * 16
     square_tasks = plan(key, left, square_out, groups, per_dev, slots, chunks)
-    cube_left, cube_right, cube_out, cube_count, _ = lax.optimization_barrier(
-        (cube_left, cube_right, cube_out, cube_count, column[1])
-    )
     from_col, left = moved_left(cube_left)
     left = left - jnp.where(from_col == 0, 0, layers * per_dev)
     key = jnp.where(from_col == 0, 0, groups) + moved_right(cube_right)
@@ -284,15 +290,22 @@
     cube_tasks = plan(key, left, cube_out, 2 * groups, groups, slots, chunks)
 
     total, panel, first = tile_sum(
-        square_tasks, 0, 2, lefts, column[:2], None, [], None, False, slots, width, 0
+        square_tasks, 0, 1, lefts, column[:1], None, [], None, False, slots, width, 0
     )
     weights = [first]
-    for seg in range(2, rows):
+    for seg in range(1, len(column), 2):
+        last = rows % 2 == 1 and seg + 2 == rows
         *result, piece = tile_sum(
-            square_tasks, seg, 1, [], [column[seg]], panel, [], total, seg == rows - 1,
+            square_tasks, seg, 2, [], column[seg : seg + 2], panel, [], total, last,
             slots, width, seg * per_dev,
         )
         total = result[0]
+        weights.append(piece)
+    if rows % 2 == 0:
+        *result, piece = tile_sum(
+            square_tasks, rows - 1, 1, [], [opposite], panel, [], total, True,
+            slots, width, (rows - 1) * per_dev,
+        )
         weights.append(piece)
     mine, other = result
     weights = jnp.concatenate(weights, axis=0)

time: 63.4 us -> 57.4 us (0.905); the launches traced: 63.5 us -> 56.4 us
  Pallas kernels: 31.6 us -> 19.5 us
  starting transfers between devices: 5.94 us -> 17.7 us
  waiting for transfers between devices: 14.8 us -> 8.08 us
    pallas_call x5, Pallas kernels: 31.6 us -> 19.5 us  [tile_sum(): pl.pallas_call(lambda *refs: body(refs), out_shape=shapes, in_specs=in_sp...]
    ppermute x11, starting transfers between devices: 5.94 us -> 17.7 us  [ring(): lax.ppermute(value, axis, [(i, (i + step) % size) for i in range(size)])]
    ppermute x11, waiting for transfers between devices: 14.8 us -> 8.08 us  [ring(): lax.ppermute(value, axis, [(i, (i + step) % size) for i in range(size)])]
  transfers between devices with their start and end apart: 11 -> 11, of which waited for: 6 -> 7; matrix products, arithmetic and copies ran while one was open for 12% -> 14% of each run, Pallas kernels for 31% -> 21%
where the time goes in v3:
time: 57.4 us; the launch traced here: 56.4 us
  Pallas kernels  19.5 us (34%)
  starting transfers between devices  17.7 us (31%)
  waiting for transfers between devices  8.08 us (14%)
  other arithmetic  8.04 us (14%)
  local copies, waits for them, and re-layouts  1.6 us (3%)
  between operations  1.48 us (3%)
    pallas_call x5, Pallas kernels, tile_sum(): pl.pallas_call(lambda *refs: body(refs), out_shape=shapes, in_specs=in_sp...  19.5 us
    ppermute x11, starting transfers between devices, ring(): lax.ppermute(value, axis, [(i, (i + step) % size) for i in range(size)])  17.7 us
    ppermute x11, waiting for transfers between devices, ring(): lax.ppermute(value, axis, [(i, (i + step) % size) for i in range(size)])  8.08 us
    reduce_sum x2, other arithmetic, plan(): jnp.sum(jnp.where(position[:, None] == slot[None, :], (left * (slots + 1)...  2.24 us
    unnamed x4, local copies, waits for them, and re-layouts  1.29 us
  transfers between devices with their start and end apart: 11, of which 7 were waited for; matrix products, arithmetic and copies ran while one was open for 14% of the time, Pallas kernels for 21%

profile of v3, /device:TPU:0, one launch (start us, length us, event | category | flops | bytes accessed | tf_op | source)
XLA Modules:
  0.0 56.4 jit_solution(8154487802274127494)
XLA Ops:
  0.0 3.0 %collective-permute-start = (f32[16,4096]{1,0:T(8,128)}, f32[16,4096]{1,0:T(8,128)S(1)}, u32[]{:S(2)}, u32[]{:S(2)}) collective-permute-start(f32[16,4096]{1,0:T(8,128)} %refs_9_.1), channel_id=1, source_target_pairs={{0,4},{4,8},{8,12},{12,0},{1,5},{5,9},{9,13},{13,1},{2,6},{6,10},{... | collective-permute-start | bytes 786440 | tf_op jit(solution)/shard_map/ppermute | solution.py:18
  3.0 0.0 collective-permute-start.2
  3.0 1.5 %collective-permute-start.3 = (f32[16,4096]{1,0:T(8,128)}, f32[16,4096]{1,0:T(8,128)S(1)}, u32[]{:S(2)}, u32[]{:S(2)}) collective-permute-start(f32[16,4096]{1,0:T(8,128)} %refs_9_.1), channel_id=1, source_target_pairs={{0,2},{2,0},{1,3},{3,1},{4,6},{6,4},{5,7},{7,5},{8,10},{10,8},{9,1... | collective-permute-start | bytes 786440 | tf_op jit(solution)/shard_map/ppermute | solution.py:18
  4.5 2.2 %collective-permute-start.5 = (f32[16,4096]{1,0:T(8,128)}, f32[16,4096]{1,0:T(8,128)S(1)}, u32[]{:S(2)}, u32[]{:S(2)}) collective-permute-start(f32[16,4096]{1,0:T(8,128)} %refs_9_.1), channel_id=1, source_target_pairs={{0,12},{4,0},{8,4},{12,8},{1,13},{5,1},{9,5},{13,9},{2,14},{6,2},{... | collective-permute-start | bytes 786440 | tf_op jit(solution)/shard_map/ppermute | solution.py:18
  7.4 0.8 %fusion.49 = (s32[1024]{0:T(1024)S(1)}, s32[1024]{0:T(1024)S(1)}, s32[1024]{0:T(1024)S(1)}) fusion(s32[1024]{0:T(1024)} %param.16, s32[1024]{0:T(1024)} %param.14, s32[]{:T(128)S(6)} %axis_index.38, s32[]{:T(128)S(6)} %axis_index.36, s32[1024]{0:T(1024)} %param.15, s32[]{:T(128)S(6)} %axis_index.33, s32[]{:T(128)} %bitcast.4, s32[1024]{0:T(1024)} %param.12, ...), kind=kLoop, calls=%fused_computation.126 | loop fusion | flops 174080 | bytes 32784 | tf_op jit(solution)/shard_map/sub | solution.py:52
  8.2 0.2 convert_reduce_fusion.2
  8.4 0.4 convert_reduce_fusion
  9.5 0.7 %fusion.14 = s32[1024]{0:T(1024)S(1)} fusion(s32[1024]{0:T(1024)} %param.11, s32[]{:T(128)S(6)} %axis_index.33, s32[]{:T(128)} %bitcast.2), kind=kLoop, calls=%fused_computation.91 | loop fusion | flops 39936 | bytes 8200 | tf_op jit(solution)/shard_map/jit(_where)/select_n | solution.py:282
  10.2 0.1 convert_reduce_fusion.3
  10.4 0.4 convert_reduce_fusion.1
  10.8 0.1 sub.189
  10.9 0.1 fusion.61
  11.0 0.1 fusion.59.refs_0_
  11.1 0.1 select_reduce_fusion.4
  11.2 0.1 fusion.60
  11.3 0.4 select_reduce_fusion.2
  11.7 0.1 sub.165
  11.8 0.1 fusion.57
  11.9 0.1 select_reduce_fusion.7.refs_0_
  12.0 0.1 select_reduce_fusion.5
  12.1 0.1 select_reduce_fusion.6
  12.2 0.1 select_reduce_fusion.3
  12.3 1.2 %select_reduce_fusion = s32[2176]{0:T(1024)S(1)} fusion(s32[1024]{0:T(1024)S(1)} %get-tuple-element.35, s32[1024]{0:T(1024)S(1)} %add_select_fusion.16), kind=kLoop, calls=%fused_computation | loop fusion | flops 6682496 | bytes 16896 | tf_op jit(solution)/shard_map/reduce_sum | solution.py:50
  13.6 0.7 %add_select_fusion.17 = s32[1024]{0:T(1024)S(1)} fusion(s32[1024]{0:T(1024)S(1)} %select_reduce_fusion.3, s32[1024]{0:T(1024)S(1)} %convert_reduce_fusion.1, s32[1024]{0:T(1024)} %param.11, s32[]{:T(128)S(6)} %axis_index.33, s32[]{:T(128)} %bitcast.3), kind=kLoop, calls=%fused_computation.132 | loop fusion | flops 43008 | bytes 16392 | tf_op jit(solution)/shard_map/jit(_where)/select_n | solution.py:48
  14.3 1.0 %select_reduce_fusion.1 = s32[1792]{0:T(1024)S(1)} fusion(s32[1024]{0:T(1024)S(1)} %get-tuple-element.45, s32[1024]{0:T(1024)S(1)} %add_select_fusion.17), kind=kLoop, calls=%fused_computation.2 | loop fusion | flops 5503232 | bytes 15360 | tf_op jit(solution)/shard_map/reduce_sum | solution.py:50
  15.3 0.0 collective-permute-done.refs_5_
  15.3 0.1 collective-permute-start.1
  15.4 0.0 collective-permute-done.3.refs_7_
  15.4 0.1 collective-permute-start.4
  15.5 0.1 convert_reduce_fusion.5.refs_2_
  15.6 0.0 collective-permute-done.2.refs_6_
  15.6 1.4 %collective-permute-done.4.refs_8_ = f32[16,4096]{1,0:T(8,128)S(1)} collective-permute-done((f32[16,4096]{1,0:T(8,128)S(1)}, f32[16,4096]{1,0:T(8,128)S(1)}, u32[]{:S(2)}, u32[]{:S(2)}) %collective-permute-start.4) | collective-permute-done | bytes 262176 | tf_op jit(solution)/shard_map/ppermute | solution.py:18
  17.0 0.0 copy-start
  17.0 0.9 %copy-done = f32[16,4096]{1,0:T(8,128)S(1)} copy-done((f32[16,4096]{1,0:T(8,128)S(1)}, f32[16,4096]{1,0:T(8,128)}, u32[]{:S(2)}) %copy-start) | copy-done | bytes 262168
  17.9 3.2 %shard_map.91 = (f32[1056,128]{1,0:T(8,128)S(1)}, bf16[2048,256]{1,0:T(8,128)(2,1)S(1)}, bf16[16,2,128,128]{3,2,1,0:T(8,128)(2,1)S(1)}) custom-call(s32[4]{0:T(128)S(1)} %select_reduce_fusion.7.refs_0_, s32[4]{0:T(128)S(1)} %and_select_fusion.6.refs_1_, s32[224]{0:T(256)S(1)} %convert_reduce_fusion.5.refs_2_, s32[1792]{0:T(1024)S(1)} %get-tuple-element.34.refs_3_, ...), custom_call_target="tpu_custom_call" | custom-call | tf_op jit(solution)/shard_map/pallas_call | solution.py:226
  21.2 0.0 collective-permute-done.5.refs_6_
  21.2 3.6 %shard_map.92 = (f32[1056,128]{1,0:T(8,128)S(1)}, bf16[32,2,128,128]{3,2,1,0:T(8,128)(2,1)S(1)}) custom-call(s32[4]{0:T(128)S(1)} %select_reduce_fusion.7.refs_0_, s32[4]{0:T(128)S(1)} %and_select_fusion.6.refs_1_, s32[224]{0:T(256)S(1)} %convert_reduce_fusion.5.refs_2_, s32[1792]{0:T(1024)S(1)} %get-tuple-element.34.refs_3_, ...), custom_call_target="tpu_custom_call" | custom-call | tf_op jit(solution)/shard_map/pallas_call | solution.py:226
  24.8 0.5 collective-permute-done.1.refs_5_
  25.3 2.8 %shard_map.93 = (f32[16,4096]{1,0:T(8,128)S(1)}, f32[16,4096]{1,0:T(8,128)S(1)}, bf16[16,2,128,128]{3,2,1,0:T(8,128)(2,1)S(1)}) custom-call(s32[4]{0:T(128)S(1)} %select_reduce_fusion.7.refs_0_, s32[4]{0:T(128)S(1)} %and_select_fusion.6.refs_1_, s32[224]{0:T(256)S(1)} %convert_reduce_fusion.5.refs_2_, s32[1792]{0:T(1024)S(1)} %get-tuple-element.34.refs_3_, ...), custom_call_target="tpu_custom_call" | custom-call | tf_op jit(solution)/shard_map/pallas_call | solution.py:226
  28.1 5.9 %collective-permute-start.6 = (f32[16,4096]{1,0:T(8,128)S(1)}, f32[16,4096]{1,0:T(8,128)S(1)}, u32[]{:S(2)}, u32[]{:S(2)}) collective-permute-start(f32[16,4096]{1,0:T(8,128)S(1)} %get-tuple-element.22), channel_id=1, source_target_pairs={{0,1},{1,0},{2,3},{3,2},{4,5},{5,4},{6,7},{7,6},{8,9},{9,8},{10,11... | collective-permute-start | bytes 786440 | tf_op jit(solution)/shard_map/ppermute | solution.py:18
  34.0 0.1 convert_reduce_fusion.4.refs_2_
  34.2 0.1 constant_dynamic-update-slice_fusion.2
  34.2 0.9 %collective-permute-done.6 = f32[16,4096]{1,0:T(8,128)S(1)} collective-permute-done((f32[16,4096]{1,0:T(8,128)S(1)}, f32[16,4096]{1,0:T(8,128)S(1)}, u32[]{:S(2)}, u32[]{:S(2)}) %collective-permute-start.6) | collective-permute-done | bytes 262176 | tf_op jit(solution)/shard_map/ppermute | solution.py:18
  35.2 0.4 collective-permute-start.7
  35.6 0.0 collective-permute-start.8
  35.6 0.3 constant_dynamic-update-slice_fusion.1
  35.9 0.1 constant_dynamic-update-slice_fusion.refs_7_
  36.1 0.7 %collective-permute-done.7.refs_6_ = f32[16,4096]{1,0:T(8,128)S(1)} collective-permute-done((f32[16,4096]{1,0:T(8,128)S(1)}, f32[16,4096]{1,0:T(8,128)S(1)}, u32[]{:S(2)}, u32[]{:S(2)}) %collective-permute-start.7) | collective-permute-done | bytes 262176 | tf_op jit(solution)/shard_map/ppermute | solution.py:18
  36.8 5.0 %shard_map.94 = (f32[1056,128]{1,0:T(8,128)S(1)}, bf16[1024,256]{1,0:T(8,128)(2,1)}) custom-call(s32[2]{0:T(128)S(1)} %fusion.59.refs_0_, s32[2]{0:T(128)S(1)} %and_select_fusion.2.refs_1_, s32[272]{0:T(512)S(1)} %convert_reduce_fusion.4.refs_2_, s32[2176]{0:T(1024)S(1)} %get-tuple-element.32.refs_3_, s32[2176]{0:T(1024)S(1)} %get-tuple-element.31.refs_4_, ...), custom_call_target="tpu_custom_call" | custom-call | tf_op jit(solution)/shard_map/pallas_call | solution.py:226
  41.8 2.2 %collective-permute-done.8.refs_5_ = f32[16,4096]{1,0:T(8,128)S(1)} collective-permute-done((f32[16,4096]{1,0:T(8,128)S(1)}, f32[16,4096]{1,0:T(8,128)S(1)}, u32[]{:S(2)}, u32[]{:S(2)}) %collective-permute-start.8) | collective-permute-done | bytes 262176 | tf_op jit(solution)/shard_map/ppermute | solution.py:18
  44.0 1.4 %collective-permute-start.9 = (f32[16,4096]{1,0:T(8,128)S(1)}, f32[16,4096]{1,0:T(8,128)S(1)}, u32[]{:S(2)}, u32[]{:S(2)}) collective-permute-start(f32[16,4096]{1,0:T(8,128)S(1)} %collective-permute-done.8.refs_5_), channel_id=1, source_target_pairs={{0,1},{1,0},{2,3},{3,2},{4,5},{5,4},{6,7},{7,6},{8,9},{9,8},{10,11... | collective-permute-start | bytes 786440 | tf_op jit(solution)/shard_map/ppermute | solution.py:18
  45.4 1.2 %collective-permute-done.9.refs_6_ = f32[16,4096]{1,0:T(8,128)S(1)} collective-permute-done((f32[16,4096]{1,0:T(8,128)S(1)}, f32[16,4096]{1,0:T(8,128)S(1)}, u32[]{:S(2)}, u32[]{:S(2)}) %collective-permute-start.9) | collective-permute-done | bytes 262176 | tf_op jit(solution)/shard_map/ppermute | solution.py:18
  46.5 4.9 %shard_map.95 = (f32[16,4096]{1,0:T(8,128)S(1)}, f32[16,4096]{1,0:T(8,128)S(1)}, bf16[1024,256]{1,0:T(8,128)(2,1)}) custom-call(s32[2]{0:T(128)S(1)} %fusion.59.refs_0_, s32[2]{0:T(128)S(1)} %and_select_fusion.2.refs_1_, s32[272]{0:T(512)S(1)} %convert_reduce_fusion.4.refs_2_, s32[2176]{0:T(1024)S(1)} %get-tuple-element.32.refs_3_, ...), custom_call_target="tpu_custom_call" | custom-call | tf_op jit(solution)/shard_map/pallas_call | solution.py:226
  51.5 3.0 %collective-permute-start.10 = (f32[16,4096]{1,0:T(8,128)S(1)}, f32[16,4096]{1,0:T(8,128)S(1)}, u32[]{:S(2)}, u32[]{:S(2)}) collective-permute-start(f32[16,4096]{1,0:T(8,128)S(1)} %get-tuple-element.30), channel_id=1, source_target_pairs={{0,1},{1,0},{2,3},{3,2},{4,5},{5,4},{6,7},{7,6},{8,9},{9,8},{10,11... | collective-permute-start | bytes 786440 | tf_op jit(solution)/shard_map/ppermute | solution.py:18
  54.5 1.2 %collective-permute-done.10 = f32[16,4096]{1,0:T(8,128)S(1)} collective-permute-done((f32[16,4096]{1,0:T(8,128)S(1)}, f32[16,4096]{1,0:T(8,128)S(1)}, u32[]{:S(2)}, u32[]{:S(2)}) %collective-permute-start.10) | collective-permute-done | bytes 262176 | tf_op jit(solution)/shard_map/ppermute | solution.py:18
  55.6 0.7 %multiply_subtract_fusion = f32[16,4096]{1,0:T(8,128)} fusion(f32[16,4096]{1,0:T(8,128)S(1)} %get-tuple-element.29, f32[16,4096]{1,0:T(8,128)S(1)} %collective-permute-done.10, f32[16,4096]{1,0:T(8,128)S(1)} %add.270.refs_5_), kind=kLoop, calls=%fused_computation.12 | loop fusion | flops 262144 | bytes 1048576 | tf_op jit(solution)/shard_map/sub | solution.py:325
  (11 shorter events, 0.1 us)
Async XLA Ops:
  0.0 15.3 %collective-permute-start = (f32[16,4096]{1,0:T(8,128)}, f32[16,4096]{1,0:T(8,128)S(1)}, u32[]{:S(2)}, u32[]{:S(2)}) collective-permute-start(f32[16,4096]{1,0:T(8,128)} %refs_9_.1), channel_id=1, source_target_pairs={{0,4},{4,8},{8,12},{12,0},{1,5},{5,9},{9,13},{13,1},{2,6},{6,10},{... | collective-permute-start | bytes 786440 | tf_op jit(solution)/shard_map/ppermute | solution.py:18
  3.0 12.5 %collective-permute-start.2 = (f32[16,4096]{1,0:T(8,128)}, f32[16,4096]{1,0:T(8,128)S(1)}, u32[]{:S(2)}, u32[]{:S(2)}) collective-permute-start(f32[16,4096]{1,0:T(8,128)} %refs_9_.1), channel_id=1, source_target_pairs={{0,1},{1,0},{2,3},{3,2},{4,5},{5,4},{6,7},{7,6},{8,9},{9,8},{10,11... | collective-permute-start | bytes 786440 | tf_op jit(solution)/shard_map/ppermute | solution.py:18
  3.0 12.3 %collective-permute-start.3 = (f32[16,4096]{1,0:T(8,128)}, f32[16,4096]{1,0:T(8,128)S(1)}, u32[]{:S(2)}, u32[]{:S(2)}) collective-permute-start(f32[16,4096]{1,0:T(8,128)} %refs_9_.1), channel_id=1, source_target_pairs={{0,2},{2,0},{1,3},{3,1},{4,6},{6,4},{5,7},{7,5},{8,10},{10,8},{9,1... | collective-permute-start | bytes 786440 | tf_op jit(solution)/shard_map/ppermute | solution.py:18
  4.5 16.7 %collective-permute-start.5 = (f32[16,4096]{1,0:T(8,128)}, f32[16,4096]{1,0:T(8,128)S(1)}, u32[]{:S(2)}, u32[]{:S(2)}) collective-permute-start(f32[16,4096]{1,0:T(8,128)} %refs_9_.1), channel_id=1, source_target_pairs={{0,12},{4,0},{8,4},{12,8},{1,13},{5,1},{9,5},{13,9},{2,14},{6,2},{... | collective-permute-start | bytes 786440 | tf_op jit(solution)/shard_map/ppermute | solution.py:18
  15.3 10.0 %collective-permute-start.1 = (f32[16,4096]{1,0:T(8,128)S(1)}, f32[16,4096]{1,0:T(8,128)S(1)}, u32[]{:S(2)}, u32[]{:S(2)}) collective-permute-start(f32[16,4096]{1,0:T(8,128)S(1)} %collective-permute-done.refs_5_), channel_id=1, source_target_pairs={{0,4},{4,8},{8,12},{12,0},{1,5},{5,9},{9,13},{13,1},{2,6},{6,10},{... | collective-permute-start | bytes 786440 | tf_op jit(solution)/shard_map/ppermute | solution.py:18
  15.4 1.6 %collective-permute-start.4 = (f32[16,4096]{1,0:T(8,128)S(1)}, f32[16,4096]{1,0:T(8,128)S(1)}, u32[]{:S(2)}, u32[]{:S(2)}) collective-permute-start(f32[16,4096]{1,0:T(8,128)S(1)} %collective-permute-done.3.refs_7_), channel_id=1, source_target_pairs={{0,1},{1,0},{2,3},{3,2},{4,5},{5,4},{6,7},{7,6},{8,9},{9,8},{10,11... | collective-permute-start | bytes 786440 | tf_op jit(solution)/shard_map/ppermute | solution.py:18
  17.0 1.0 %copy-start = (f32[16,4096]{1,0:T(8,128)S(1)}, f32[16,4096]{1,0:T(8,128)}, u32[]{:S(2)}) copy-start(f32[16,4096]{1,0:T(8,128)} %refs_9_.1) | copy-start | bytes 786436
  28.1 7.1 %collective-permute-start.6 = (f32[16,4096]{1,0:T(8,128)S(1)}, f32[16,4096]{1,0:T(8,128)S(1)}, u32[]{:S(2)}, u32[]{:S(2)}) collective-permute-start(f32[16,4096]{1,0:T(8,128)S(1)} %get-tuple-element.22), channel_id=1, source_target_pairs={{0,1},{1,0},{2,3},{3,2},{4,5},{5,4},{6,7},{7,6},{8,9},{9,8},{10,11... | collective-permute-start | bytes 786440 | tf_op jit(solution)/shard_map/ppermute | solution.py:18
  35.2 1.6 %collective-permute-start.7 = (f32[16,4096]{1,0:T(8,128)S(1)}, f32[16,4096]{1,0:T(8,128)S(1)}, u32[]{:S(2)}, u32[]{:S(2)}) collective-permute-start(f32[16,4096]{1,0:T(8,128)S(1)} %add.270.refs_5_), channel_id=1, source_target_pairs={{0,1},{1,0},{2,3},{3,2},{4,5},{5,4},{6,7},{7,6},{8,9},{9,8},{10,11... | collective-permute-start | bytes 786440 | tf_op jit(solution)/shard_map/ppermute | solution.py:18
  35.6 8.3 %collective-permute-start.8 = (f32[16,4096]{1,0:T(8,128)S(1)}, f32[16,4096]{1,0:T(8,128)S(1)}, u32[]{:S(2)}, u32[]{:S(2)}) collective-permute-start(f32[16,4096]{1,0:T(8,128)S(1)} %add.270.refs_5_), channel_id=1, source_target_pairs={{0,2},{2,0},{1,3},{3,1},{4,6},{6,4},{5,7},{7,5},{8,10},{10,8},{9,1... | collective-permute-start | bytes 786440 | tf_op jit(solution)/shard_map/ppermute | solution.py:18
  44.0 2.5 %collective-permute-start.9 = (f32[16,4096]{1,0:T(8,128)S(1)}, f32[16,4096]{1,0:T(8,128)S(1)}, u32[]{:S(2)}, u32[]{:S(2)}) collective-permute-start(f32[16,4096]{1,0:T(8,128)S(1)} %collective-permute-done.8.refs_5_), channel_id=1, source_target_pairs={{0,1},{1,0},{2,3},{3,2},{4,5},{5,4},{6,7},{7,6},{8,9},{9,8},{10,11... | collective-permute-start | bytes 786440 | tf_op jit(solution)/shard_map/ppermute | solution.py:18
  51.5 4.2 %collective-permute-start.10 = (f32[16,4096]{1,0:T(8,128)S(1)}, f32[16,4096]{1,0:T(8,128)S(1)}, u32[]{:S(2)}, u32[]{:S(2)}) collective-permute-start(f32[16,4096]{1,0:T(8,128)S(1)} %get-tuple-element.30), channel_id=1, source_target_pairs={{0,1},{1,0},{2,3},{3,2},{4,5},{5,4},{6,7},{7,6},{8,9},{9,8},{10,11... | collective-permute-start | bytes 786440 | tf_op jit(solution)/shard_map/ppermute | solution.py:18
